TPU v7x, 256 devices: a whole 4x4x8 slice. The times are simulated.
256 devices in a mesh: ctx: 64 (over z, y_hi, x), tp: 4 (over y_lo, core).
Axes of the slice: x: 4, y: 4 (y_hi: 2, y_lo: 2; y = y_hi * 2 + y_lo), z: 8, core: 2. Of those that a mesh axis runs over, the one named last changes fastest.
Arguments:
- span_q: bfloat16 [8192, 32, 128], P('ctx', 'tp'), may hold values from -104 to 104
- cache_kv: bfloat16 [8192, 8, 2, 128], P('ctx', 'tp'), may hold values from -4 to 4
- span_kv: bfloat16 [8192, 8, 2, 128], P('ctx', 'tp'), may hold values from -4 to 4
- span_blocks: int32 [64], replicated, may hold values from 0 to 63, each once
- parked_pages: bfloat16 [4096, 8, 8, 2, 128], P('ctx', None, 'tp'), may hold values from -4 to 4
- page_dest: int32 [4096, 1], replicated, may hold values from 0 to 63; in each aligned block of 64 rows (0 to 63, 64 to 127, ...) at most 2 rows name the same one
- page_req: int32 [4096], replicated, may hold values from 0 to 3
- decode_cache: bfloat16 [256, 512, 8, 2, 128], P('ctx', None, 'tp'), may hold values from -4 to 4
- decode_lengths: int32 [256], P('ctx'), may hold values from 1 to 512, 65536 in all
- decode_q: bfloat16 [256, 4, 32, 128], P('ctx', None, 'tp'), may hold values from -104 to 104
- decode_kv: bfloat16 [256, 4, 8, 2, 128], P('ctx', None, 'tp'), may hold values from -4 to 4
- out_weight: bfloat16 [32, 128, 4096], P('tp'), may hold values from -0.09375 to 0.09375
Outputs:
- prefill_out: bfloat16 [8192, 4096], P(('ctx', 'tp'))
- decode_out: bfloat16 [256, 4, 4096], P(('ctx', 'tp'))
Inputs may be any that keep to these rules, and one draw needn't show every extreme that they name: `page_dest`: at most 2 of the 64 pages of one index of ctx name the same destination.
All inputs are finite; a program needn't handle non-finite values. No bound on the sum of `decode_lengths` on one device may be relied on, other than what follows from the above.
Results may differ from a plain program's by a relative error of at most 0.015.
Values may be sent and summed in bfloat16 or wider, within the bound.
A program may use at most 128 MiB of HBM per device.

v0:
```python
import math

import jax
import jax.numpy as jnp
from jax import lax
from jax.sharding import PartitionSpec as P

NEG = -1e30


def pick_entry(table, where_at):
    slots = jnp.arange(table.shape[0], dtype=jnp.int32)
    return jnp.sum(jnp.where(where_at[..., None] == slots, table, 0), axis=-1)


def body(
    span_q,
    cache_kv,
    span_kv,
    span_blocks,
    parked_pages,
    page_dest,
    page_req,
    decode_cache,
    decode_lengths,
    decode_q,
    decode_kv,
    out_weight,
):
    ctx_count = lax.axis_size("ctx")
    tp_count = lax.axis_size("tp")
    own_index = lax.axis_index("ctx")
    ch_rows, heads_loc, head_dim = span_q.shape
    cache_rows = cache_kv.shape[0]
    kv_loc = cache_kv.shape[1]
    group_size = heads_loc // kv_loc
    score_scale = head_dim ** (-0.5)
    row_ids = jnp.arange(ch_rows, dtype=jnp.int32)
    query_pos = pick_entry(span_blocks, own_index) * ch_rows + row_ids

    def span_pos(source, local_row):
        return pick_entry(span_blocks, source) * ch_rows + local_row

    grouped_q = span_q.reshape(ch_rows, kv_loc, group_size, head_dim)

    def attend_tile(softmax_state, key_block, key_pos):
        running_max, denominator, numerator = softmax_state
        key_rows = key_block[:, :, 0, :]
        value_rows = key_block[:, :, 1, :]
        scores = (
            jnp.einsum("tkgd,nkd->kgtn", grouped_q, key_rows, preferred_element_type=jnp.float32)
            * score_scale
        )
        visible = key_pos[None, :] <= query_pos[:, None]
        scores = jnp.where(visible, scores, NEG)
        new_max = jnp.maximum(running_max, jnp.max(scores, axis=-1))
        weights = jnp.where(visible, jnp.exp(scores - new_max[..., None]), 0.0)
        shrink = jnp.exp(running_max - new_max)
        denominator = denominator * shrink + jnp.sum(weights, axis=-1)
        numerator = numerator * shrink[..., None] + jnp.einsum(
            "kgtn,nkd->kgtd",
            weights.astype(jnp.bfloat16),
            value_rows,
            preferred_element_type=jnp.float32,
        )
        return (new_max, denominator, numerator)

    def make_fold(shard_rows, position_of, softmax_state, kv_piece):
        row_count = kv_piece.shape[0]
        tile_rows = math.gcd(row_count, 1024)
        tiles = kv_piece.reshape(row_count // tile_rows, tile_rows, kv_loc, 2, head_dim)
        tile_starts = jnp.arange(row_count // tile_rows, dtype=jnp.int32) * tile_rows

        def scan_step(state_in, scan_item):
            key_block, tile_first = scan_item
            key_index = tile_first + jnp.arange(tile_rows, dtype=jnp.int32)
            key_pos = position_of(key_index // shard_rows, key_index % shard_rows)
            state_out = attend_tile(state_in, key_block, key_pos)
            return (state_out, None)

        result, _ = lax.scan(scan_step, softmax_state, (tiles, tile_starts))
        return result

    def cache_position(source, local_row):
        return jnp.full(local_row.shape, -1, jnp.int32)

    start_state = (
        jnp.full((kv_loc, group_size, ch_rows), NEG, jnp.float32),
        jnp.zeros((kv_loc, group_size, ch_rows), jnp.float32),
        jnp.zeros((kv_loc, group_size, ch_rows, head_dim), jnp.float32),
    )
    cache_state = make_fold(
        cache_rows, cache_position, start_state, lax.all_gather(cache_kv, "ctx", axis=0, tiled=True)
    )
    final_state = make_fold(
        ch_rows, span_pos, cache_state, lax.all_gather(span_kv, "ctx", axis=0, tiled=True)
    )
    attention = (final_state[2] / final_state[1][..., None]).astype(jnp.bfloat16)
    attention = jnp.transpose(attention, (2, 0, 1, 3)).reshape(ch_rows, heads_loc, head_dim)
    weight = out_weight.reshape(heads_loc * head_dim, out_weight.shape[2])
    flat_attn = attention.reshape(ch_rows, heads_loc * head_dim)
    prefill_out = lax.psum_scatter(
        jnp.dot(flat_attn, weight, preferred_element_type=jnp.float32).astype(jnp.bfloat16),
        "tp",
        scatter_dimension=0,
        tiled=True,
    )
    page_tokens = parked_pages.shape[1]
    pages_dev = parked_pages.shape[0]
    page_width = page_tokens * kv_loc * 2 * head_dim
    local_pages = parked_pages.reshape(pages_dev, page_width)
    slot_depth = max(2, (2 * pages_dev + ctx_count - 1) // ctx_count)
    targets = page_dest[:, 0].reshape(ctx_count, pages_dev)
    page_hits = (
        targets[:, :, None] == jnp.arange(ctx_count, dtype=jnp.int32)[None, None, :]
    ).astype(jnp.int32)
    earlier = jnp.cumsum(page_hits, axis=1) - page_hits
    page_rank = jnp.sum(earlier * page_hits, axis=2)
    own_targets = lax.dynamic_index_in_dim(targets, own_index, 0, keepdims=False)
    own_rank = lax.dynamic_index_in_dim(page_rank, own_index, 0, keepdims=False)
    send_slot = own_targets * slot_depth + own_rank
    selector = (
        jnp.arange(ctx_count * slot_depth, dtype=jnp.int32)[:, None] == send_slot[None, :]
    ).astype(jnp.bfloat16)
    outgoing = jnp.dot(selector, local_pages, preferred_element_type=jnp.float32).astype(
        jnp.bfloat16
    )
    incoming = lax.all_to_all(
        outgoing.reshape(ctx_count, slot_depth, page_width),
        "ctx",
        split_axis=0,
        concat_axis=0,
        tiled=True,
    )
    pool_rows = incoming.reshape(ctx_count * slot_depth * page_tokens, kv_loc, 2, head_dim)
    to_here = targets == own_index
    match_slot = to_here[:, :, None] & (
        page_rank[:, :, None] == jnp.arange(slot_depth, dtype=jnp.int32)[None, None, :]
    )
    request_tag = page_req.reshape(ctx_count, pages_dev)[:, :, None] + 1
    slot_owner = jnp.sum(jnp.where(match_slot, request_tag, 0), axis=1).reshape(-1)
    pool_owner = jnp.broadcast_to(slot_owner[:, None], (slot_owner.shape[0], page_tokens)).reshape(
        -1
    )
    req_count, steps_count = (decode_q.shape[0], decode_q.shape[1])
    res_len = decode_cache.shape[1]
    dec_query = decode_q.reshape(req_count, steps_count, kv_loc, group_size, head_dim)
    res_scores = (
        jnp.einsum(
            "rskgd,rnkd->rkgsn",
            dec_query,
            decode_cache[:, :, :, 0, :],
            preferred_element_type=jnp.float32,
        )
        * score_scale
    )
    pool_scores = (
        jnp.einsum(
            "rskgd,nkd->rkgsn", dec_query, pool_rows[:, :, 0, :], preferred_element_type=jnp.float32
        )
        * score_scale
    )
    new_scores = (
        jnp.einsum(
            "rskgd,rukd->rkgsu",
            dec_query,
            decode_kv[:, :, :, 0, :],
            preferred_element_type=jnp.float32,
        )
        * score_scale
    )
    seen_res = (jnp.arange(res_len, dtype=jnp.int32)[None, :] < decode_lengths[:, None])[
        :, None, None, None, :
    ]
    seen_pool = (pool_owner[None, :] == jnp.arange(1, req_count + 1, dtype=jnp.int32)[:, None])[
        :, None, None, None, :
    ]
    step_ids = jnp.arange(steps_count, dtype=jnp.int32)
    seen_new = (step_ids[None, :] <= step_ids[:, None])[None, None, None, :, :]
    res_scores = jnp.where(seen_res, res_scores, NEG)
    pool_scores = jnp.where(seen_pool, pool_scores, NEG)
    new_scores = jnp.where(seen_new, new_scores, NEG)
    peak = jnp.maximum(
        jnp.maximum(jnp.max(res_scores, axis=-1), jnp.max(pool_scores, axis=-1)),
        jnp.max(new_scores, axis=-1),
    )
    res_weights = jnp.where(seen_res, jnp.exp(res_scores - peak[..., None]), 0.0)
    pool_weights = jnp.where(seen_pool, jnp.exp(pool_scores - peak[..., None]), 0.0)
    new_weights = jnp.where(seen_new, jnp.exp(new_scores - peak[..., None]), 0.0)
    denominator = (
        jnp.sum(res_weights, axis=-1)
        + jnp.sum(pool_weights, axis=-1)
        + jnp.sum(new_weights, axis=-1)
    )
    numerator = jnp.einsum(
        "rkgsn,rnkd->rkgsd",
        res_weights.astype(jnp.bfloat16),
        decode_cache[:, :, :, 1, :],
        preferred_element_type=jnp.float32,
    )
    numerator = numerator + jnp.einsum(
        "rkgsn,nkd->rkgsd",
        pool_weights.astype(jnp.bfloat16),
        pool_rows[:, :, 1, :],
        preferred_element_type=jnp.float32,
    )
    numerator = numerator + jnp.einsum(
        "rkgsu,rukd->rkgsd",
        new_weights.astype(jnp.bfloat16),
        decode_kv[:, :, :, 1, :],
        preferred_element_type=jnp.float32,
    )
    decode_attn = (numerator / denominator[..., None]).astype(jnp.bfloat16)
    decode_attn = jnp.transpose(decode_attn, (0, 3, 1, 2, 4)).reshape(
        req_count, steps_count, heads_loc * head_dim
    )
    row_count = req_count // tp_count * lax.axis_size("tp")
    picked = decode_attn.reshape(row_count * steps_count, heads_loc * head_dim)
    decode_out = lax.psum_scatter(
        jnp.dot(picked, weight, preferred_element_type=jnp.float32)
        .reshape(row_count, steps_count, weight.shape[1])
        .astype(jnp.bfloat16),
        "tp",
        scatter_dimension=0,
        tiled=True,
    )
    return (prefill_out, decode_out)


def solution(mesh):
    return jax.shard_map(
        body,
        mesh=mesh,
        in_specs=(
            P("ctx", "tp", None),
            P("ctx", "tp", None, None),
            P("ctx", "tp", None, None),
            P(),
            P("ctx", None, "tp", None, None),
            P(),
            P(),
            P("ctx", None, "tp", None, None),
            P("ctx"),
            P("ctx", None, "tp", None),
            P("ctx", None, "tp", None, None),
            P("tp", None, None),
        ),
        out_specs=(P(("ctx", "tp"), None), P(("ctx", "tp"), None, None)),
        check_vma=False,
    )
```

profile of v0, /device:TPU:1, one launch (start us, length us, event | category | flops | bytes accessed | tf_op | source)
XLA Modules:
  0.0 402.4 jit_solution(10471380908133140941)
XLA Ops:
  11.3 2.4 reshape.170
  15.8 2.3 fusion.42
  21.2 15.4 %all-to-all-start = ((bf16[64,2,4096]{2,1,0:T(2,128)(2,1)}), bf16[64,2,4096]{2,1,0:T(2,128)(2,1)}, u32[]{:S(2)}, u32[]{:S(2)}) async-start(bf16[64,2,4096]{2,1,0:T(2,128)(2,1)} %reshape.171), calls=%async_computation.1 | async-start | bytes 2097152 | tf_op jit(solution)/shard_map/all_to_all | solution.py:128
  42.0 3.8 fusion.71
  47.0 18.6 %all-to-all-done = bf16[64,2,4096]{2,1,0:T(2,128)(2,1)} async-done(((bf16[64,2,4096]{2,1,0:T(2,128)(2,1)}), bf16[64,2,4096]{2,1,0:T(2,128)(2,1)}, u32[]{:S(2)}, u32[]{:S(2)}) %all-to-all-start) | async-done | bytes 1048608 | tf_op jit(solution)/shard_map/all_to_all | solution.py:128
  65.6 1.9 reshape.172
  67.4 2.3 fusion.72
  74.0 2.1 fusion.54
  78.9 5.4 %convolution_convert_fusion.2 = bf16[4,4,4096]{2,1,0:T(4,128)(2,1)} fusion(bf16[4,4,1024]{2,1,0:T(4,128)(2,1)S(1)} %bitcast.214, bf16[1024,4096,1]{1,0,2:T(8,128)(2,1)} %bitcast.202), kind=kOutput, calls=%fused_computation.64 | convolution fusion | flops 134283264 | bytes 8552448 | tf_op jit(solution)/shard_map/dot_general | solution.py:220
  84.5 78.7 %all-gather.3.cloned.1.call-done = bf16[8192,2,2,128]{3,0,2,1:T(8,128)(2,1)} async-done(((bf16[128,2,2,128]{3,0,2,1:T(8,128)(2,1)}), bf16[8192,2,2,128]{3,0,2,1:T(8,128)(2,1)}) %all-gather.3.cloned.1.call-update) | async-done | bytes 8388624 | tf_op jit(solution)/shard_map/all_gather | solution.py:93
  163.2 72.1 %while.33 = (s32[]{:T(128)}, f32[2,4,128]{2,1,0:T(4,128)S(1)}, f32[2,4,128]{2,1,0:T(4,128)S(1)}, f32[2,4,128,128]{3,2,1,0:T(8,128)S(1)}, bf16[8,1024,2,2,128]{4,...) while((s32[]{:T(128)}, f32[2,4,128]{2,1,0:T(4,128)S(1)}, ...), condition=%wide.region_4.5_spmd.clone, body=%wide.region_1.4_spmd.clone.sunk | while | flops 550900992 | bytes 33884052 | solution.py:81
  164.5 2.6 bitcast_reduce_fusion.2
  167.2 3.3 fusion.105
  173.5 2.6 bitcast_reduce_fusion.2
  176.1 3.3 fusion.105
  182.5 2.6 bitcast_reduce_fusion.2
  185.1 3.3 fusion.105
  191.5 2.6 bitcast_reduce_fusion.2
  194.1 3.3 fusion.105
  200.5 2.6 bitcast_reduce_fusion.2
  203.1 3.3 fusion.105
  209.4 2.6 bitcast_reduce_fusion.2
  212.1 3.3 fusion.105
  218.5 2.6 bitcast_reduce_fusion.2
  221.2 3.3 fusion.105
  227.6 2.6 bitcast_reduce_fusion.2
  230.2 3.4 fusion.105
  235.3 75.4 %all-gather.5.cloned.1.call-done = bf16[8192,2,2,128]{3,0,2,1:T(8,128)(2,1)} async-done(((bf16[128,2,2,128]{3,0,2,1:T(8,128)(2,1)}), bf16[8192,2,2,128]{3,0,2,1:T(8,128)(2,1)}) %all-gather.5.cloned.1.call-update) | async-done | bytes 8388624 | tf_op jit(solution)/shard_map/all_gather | solution.py:96
  310.7 55.8 %while.32 = (s32[]{:T(128)}, f32[2,4,128]{2,1,0:T(4,128)S(1)}, f32[2,4,128]{2,1,0:T(4,128)S(1)}, f32[2,4,128,128]{3,2,1,0:T(8,128)S(1)}, s32[8]{0:T(128)S(1)}, /...) while((s32[]{:T(128)}, f32[2,4,128]{2,1,0:T(4,128)S(1)}, ...), condition=%wide.region_9.10_spmd.clone, body=%wide.region_5.9_spmd.clone.sunk | while | flops 551124096 | bytes 17655176 | solution.py:81
  366.8 5.7 %convolution_convert_fusion.1 = bf16[128,4096]{1,0:T(8,128)(2,1)} fusion(bf16[128,1024]{0,1:T(8,128)(2,1)S(1)} %bitcast.207, bf16[1024,4096]{1,0:T(8,128)(2,1)} %bitcast.203), kind=kOutput, calls=%fused_computation.63 | convolution fusion | flops 1074266112 | bytes 9699328 | tf_op jit(solution)/shard_map/dot_general | solution.py:103
  373.1 2.1 constant_dynamic-slice_fusion.2
  375.2 19.8 %reduce-scatter.2.cloned.1.call-done = bf16[32,4096]{1,0:T(8,128)(2,1)} async-done(((bf16[128,4096]{1,0:T(8,128)(2,1)}), bf16[32,4096]{1,0:T(8,128)(2,1)}) %reduce-scatter.2.cloned.1.call-update) | async-done | bytes 262160 | tf_op jit(solution)/shard_map/reduce_scatter | solution.py:102
  (247 shorter events, 101.7 us)
Async XLA Ops:
  8.0 33.0 %copy-start = (bf16[4,4,8,128]{3,2,1,0:T(8,128)(2,1)S(1)}, bf16[4,4,8,128]{3,2,1,0:T(8,128)(2,1)}, u32[]{:S(2)}) copy-start(bf16[4,4,8,128]{3,2,1,0:T(8,128)(2,1)} %param.25) | copy-start | bytes 98308
  8.0 155.2 %all-gather.3.cloned.1.call-start = ((), (), s32[]{:S(2)}) async-start(), calls=%async_computation.2 | async-start | bytes 8519680 | tf_op jit(solution)/shard_map/all_gather | solution.py:93
  9.6 28.1 %copy-start.7 = (s32[4096]{0:T(1024)S(1)}, s32[4096]{0:T(1024)}, u32[]{:S(2)}) copy-start(s32[4096]{0:T(1024)} %param.22) | copy-start | bytes 49156
  9.7 301.1 %all-gather.5.cloned.1.call-start = ((), (), s32[]{:S(2)}) async-start(), calls=%async_computation.3 | async-start | bytes 8519680 | tf_op jit(solution)/shard_map/all_gather | solution.py:96
  11.3 27.1 %copy-start.9 = (s32[64]{0:T(128)S(1)}, s32[64]{0:T(128)}, u32[]{:S(2)}) copy-start(s32[64]{0:T(128)} %param.19) | copy-start | bytes 772
  11.3 28.9 %copy-start.11 = (s32[4]{0:T(128)S(1)}, s32[4]{0:T(128)}, u32[]{:S(2)}) copy-start(s32[4]{0:T(128)} %param.24) | copy-start | bytes 52
  11.3 29.1 %copy-start.6 = (bf16[4,4,2,2,128]{4,3,2,1,0:T(2,128)(2,1)S(1)}, bf16[4,4,2,2,128]{4,3,2,1,0:T(2,128)(2,1)}, u32[]{:S(2)}) copy-start(bf16[4,4,2,2,128]{4,3,2,1,0:T(2,128)(2,1)} %param.26) | copy-start | bytes 49156
  11.3 30.7 %copy-start.2 = (bf16[4,512,2,2,128]{4,3,2,1,0:T(2,128)(2,1)S(1)}, bf16[4,512,2,2,128]{4,3,2,1,0:T(2,128)(2,1)}, u32[]{:S(2)}) copy-start(bf16[4,512,2,2,128]{4,3,2,1,0:T(2,128)(2,1)} %param.23) | copy-start | bytes 6291460
  21.2 44.4 %all-to-all-start = ((bf16[64,2,4096]{2,1,0:T(2,128)(2,1)}), bf16[64,2,4096]{2,1,0:T(2,128)(2,1)}, u32[]{:S(2)}, u32[]{:S(2)}) async-start(bf16[64,2,4096]{2,1,0:T(2,128)(2,1)} %reshape.171), calls=%async_computation.1 | async-start | bytes 2097152 | tf_op jit(solution)/shard_map/all_to_all | solution.py:128
  36.6 336.5 %all-reduce.3.cloned.1.call-start = ((), (), s32[]{:S(2)}) async-start(), calls=%async_computation.5 | async-start | bytes 262144
  40.3 5.6 %copy-start.10 = (pred[4,512]{1,0:T(4,128)(4,1)}, pred[4,512]{1,0:T(4,128)(4,1)S(1)}, u32[]{:S(2)}) copy-start(pred[4,512]{1,0:T(4,128)(4,1)S(1)} %iota_compare_fusion.6) | copy-start | bytes 6148
  67.4 8.9 %copy-start.3 = (bf16[4,512,2,1,128]{4,3,2,1,0:T(2,128)(2,1)S(1)}, bf16[4,512,2,1,128]{4,3,2,1,0:T(2,128)(2,1)}, u32[]{:S(2)}) copy-start(bf16[4,512,2,1,128]{4,3,2,1,0:T(2,128)(2,1)} %get-tuple-element.332) | copy-start | bytes 3145732
  69.8 7.7 %copy-start.4 = (bf16[1024,2,1,128]{3,2,1,0:T(2,128)(2,1)S(1)}, bf16[1024,2,1,128]{3,2,1,0:T(2,128)(2,1)}, u32[]{:S(2)}) copy-start(bf16[1024,2,1,128]{3,2,1,0:T(2,128)(2,1)} %get-tuple-element.333) | copy-start | bytes 1572868
  72.2 6.5 %copy-start.8 = (bf16[4,4,2,1,128]{4,3,2,1,0:T(2,128)(2,1)S(1)}, bf16[4,4,2,1,128]{4,3,2,1,0:T(2,128)(2,1)}, u32[]{:S(2)}) copy-start(bf16[4,4,2,1,128]{4,3,2,1,0:T(2,128)(2,1)} %get-tuple-element.341) | copy-start | bytes 24580
  78.9 84.3 %copy-start.5 = (f32[2,4,128,128]{3,2,1,0:T(8,128)S(1)}, f32[2,4,128,128]{3,2,1,0:T(8,128)}, u32[]{:S(2)}) copy-start(f32[2,4,128,128]{3,2,1,0:T(8,128)} %custom-call.2) | copy-start | bytes 1572868
  84.3 310.7 %reduce-scatter.2.cloned.1.call-start = ((), (), s32[]{:S(2)}) async-start(), calls=%async_computation.4 | async-start | bytes 1310720 | tf_op jit(solution)/shard_map/reduce_scatter | solution.py:102
  163.2 147.5 %copy-start.13 = (s32[8]{0:T(128)S(1)}, s32[8]{0:T(128)}, u32[]{:S(2)}) copy-start(s32[8]{0:T(128)} %iota_multiply_fusion) | copy-start | bytes 100
  167.2 3.4 copy-start.1
  176.1 3.5 copy-start.1
  185.1 3.5 copy-start.1
  194.1 3.5 copy-start.1
  203.1 3.4 copy-start.1
  212.1 3.4 copy-start.1
  221.2 3.5 copy-start.1
  230.2 3.6 copy-start.1
  366.7 5.7 %copy-start.12 = (u32[256]{0:T(256)S(1)}, u32[256]{0:T(256)}, u32[]{:S(2)}) copy-start(u32[256]{0:T(256)} %constant.144) | copy-start | bytes 3076
Sparse Core Ops, SparseCore 0:
  12.9 150.2 all-gather.2
  167.3 143.4 all-gather.4
Sparse Core Ops, SparseCore 1:
  84.4 59.9 all-reduce.2
  372.5 22.4 reduce-scatter.1
where the time goes:
time: 404 us; the launch traced here: 402 us
  waiting for transfers between devices  192 us (48%)
  matrix products  70.4 us (17%)
  other arithmetic  58.3 us (14%)
  local copies, waits for them, and re-layouts  48.1 us (12%)
  between operations  16.4 us (4%)
  starting transfers between devices  15.7 us (4%)
    all_gather x1, waiting for transfers between devices, body(): lax.all_gather(cache_kv, 'ctx', axis=0, tiled=True)  78.7 us
    all_gather x1, waiting for transfers between devices, body(): lax.all_gather(span_kv, 'ctx', axis=0, tiled=True)  75.4 us
    reduce_sum x16, other arithmetic, attend_tile(): denominator = denominator * shrink + jnp.sum(weights, axis=-1)  34.7 us
    dot_general x16, matrix products, attend_tile(): jnp.einsum('tkgd,nkd->kgtn', grouped_q, key_rows, preferred_element_type=...  27.2 us
    dot_general x16, matrix products, attend_tile(): jnp.einsum('kgtn,nkd->kgtd', weights.astype(jnp.bfloat16), value_rows, pr...  24.8 us
    squeeze x16, local copies, waits for them, and re-layouts, make_fold(): result, _ = lax.scan(scan_step, softmax_state, (tiles, tile_starts))  21.1 us
    reduce_scatter x1, waiting for transfers between devices, body(): lax.psum_scatter(jnp.dot(flat_attn, weight, preferred_element_type=jnp.fl...  19.8 us
    all_to_all x1, waiting for transfers between devices, body(): lax.all_to_all(outgoing.reshape(ctx_count, slot_depth, page_width), 'ctx'...  18.6 us
  transfers between devices with their start and end apart: 5, of which 4 were waited for; matrix products, arithmetic and copies ran while one was open for 43% of the time, Pallas kernels for 0%

commit v1 on v0

v1 whole, which is shorter than its diff:
```python
import functools

import jax
import jax.numpy as jnp
from jax import lax
from jax.experimental import pallas as pl
from jax.experimental.pallas import tpu as pltpu
from jax.sharding import PartitionSpec as P

NEG = -1e30
LOG2E = 1.4426950408889634
MESH = pl.DeviceIdType.MESH
BF16 = jnp.bfloat16
F32 = jnp.float32
NT = (((1,), (1,)), ((), ()))

NZ, NR = 8, 8
TOK = 128
HD = 128
GROUP = 4
QROWS = GROUP * TOK
KEYS = 2 * TOK * NZ
COLS = 1024
CHUNKS = 4
PAGE_ROWS = 32
POOL = 4096


def remote(src, dst, send, recv, **device):
    return pltpu.make_async_remote_copy(
        src_ref=src, dst_ref=dst, send_sem=send, recv_sem=recv, device_id=device, device_id_type=MESH
    )


def fold8(x):
    return jnp.max(x.reshape(x.shape[0] // 8, 8, x.shape[1]), axis=0)


def kernel(
    blocks_ref, page_ix_ref, lens_ref, q_in, kv_in, pages_in, owner_ref, cache_in, dq_ref, dkv_ref, w_in,
    out_ref, dout_ref,
    kvbuf, qbuf, s_ref, obuf, orecv, stbuf, strecv, dbias, pages, pg_out, pool, dcache, wbuf,
    lhs, pbuf, rbuf, sbuf, tbuf, pdec, rdec, sdec, tdec,
    lsem, kv_s, kv_r, q_s, q_r, o_s, o_r, st_s, st_r, pg_s, pg_r, t1_s, t1_r, t2_s, t2_r,
):
    me = lax.axis_index("ctx")
    tp = lax.axis_index("tp")
    z = me // NR
    rest = me % NR
    score_c = (HD ** -0.5) * LOG2E

    barrier = pltpu.get_barrier_semaphore()

    def greet(k, _):
        pl.semaphore_signal(barrier, inc=1, device_id={"ctx": (me + k) % 64}, device_id_type=MESH)
        return 0

    lax.fori_loop(1, 64, greet, 0)
    for k in range(1, 4):
        pl.semaphore_signal(barrier, inc=1, device_id={"tp": (tp + k) % 4}, device_id_type=MESH)

    local = [
        pltpu.make_async_copy(kv_in, kvbuf.at[:, 0], lsem.at[0]),
        pltpu.make_async_copy(q_in, qbuf.at[0], lsem.at[1]),
        pltpu.make_async_copy(pages_in, pages, lsem.at[2]),
        pltpu.make_async_copy(cache_in, dcache, lsem.at[3]),
        pltpu.make_async_copy(w_in, wbuf, lsem.at[4]),
    ]
    for copy in local:
        copy.start()
    local[0].wait()
    local[1].wait()
    pl.semaphore_wait(barrier, 66)

    q_copies = []
    for k in range(1, NR):
        copy = remote(
            qbuf.at[0], qbuf.at[k], q_s.at[k], q_r.at[k], ctx=z * NR + (rest + k) % NR
        )
        copy.start()
        q_copies.append(copy)

    ring = {}
    order = []
    for t in range(4):
        for half in range(2):
            for way in range(2):
                if t == 3 and half != way:
                    continue
                here = (-t) % NZ if way == 0 else t
                there = (-t - 1) % NZ if way == 0 else t + 1
                to = (z + 1) % NZ if way == 0 else (z + NZ - 1) % NZ
                ring[t, half, way] = remote(
                    kvbuf.at[:, here, half], kvbuf.at[:, there, half],
                    kv_s.at[way, t, half], kv_r.at[way, t, half], ctx=to * NR + rest,
                )
                order.append((t, half, way))
    for key in order:
        if key[0] == 0:
            ring[key].start()

    local[2].wait()

    def place(t, _):
        for i in range(2):
            pg_out[t, i * PAGE_ROWS : (i + 1) * PAGE_ROWS, :] = pages[page_ix_ref[t * 2 + i]]
        return 0

    lax.fori_loop(0, 64, place, 0)

    local[3].wait()
    row = lax.broadcasted_iota(jnp.int32, (128, 128), 0)
    lane = lax.broadcasted_iota(jnp.int32, (128, 128), 1)
    perm = (lane == (row % 16) * 8 + row // 16).astype(BF16)
    dq = jnp.dot(perm, dq_ref[...], preferred_element_type=F32).astype(BF16)
    col_req = (lax.broadcasted_iota(jnp.int32, (128, 1), 0) // 4) % 4
    col_step = lax.broadcasted_iota(jnp.int32, (128, 1), 0) % 4
    col_head = lax.broadcasted_iota(jnp.int32, (128, 1), 0) // 64
    length = jnp.zeros((128, 1), jnp.int32)
    for r in range(4):
        length = jnp.where(col_req == r, lens_ref[r], length)

    def weigh(scores):
        m = jnp.max(scores, axis=1, keepdims=True)
        p = jnp.exp2(scores * score_c - m * score_c)
        total = jnp.sum(p, axis=1, keepdims=True)
        return m * score_c, total, pltpu.roll(p, 1, 1).astype(BF16)

    wide = jnp.concatenate([dcache[r * 2048 : (r + 1) * 2048, :] for r in range(4)], axis=1)
    zero = jnp.zeros((), BF16)
    dq_wide = jnp.concatenate([jnp.where(col_req == r, dq, zero) for r in range(4)], axis=1)
    res = lax.dot_general(dq_wide, wide, NT, preferred_element_type=F32)
    at = lax.broadcasted_iota(jnp.int32, (1, 2048), 1)
    res = jnp.where((at // 4 < length) & (at % 4 == col_head * 2), res, NEG)
    new = lax.dot_general(dq, dkv_ref[...], NT, preferred_element_type=F32)
    at = lax.broadcasted_iota(jnp.int32, (1, 64), 1)
    new = jnp.where(
        (at // 16 == col_req) & ((at // 4) % 4 <= col_step) & (at % 4 == col_head * 2), new, NEG
    )
    new = jnp.concatenate([new, jnp.full((128, 64), NEG, F32)], axis=1)
    res_m, res_l, res_p = weigh(jnp.concatenate([res, new], axis=1))
    part = jnp.dot(res_p[:, :2048], wide, preferred_element_type=F32)
    res_o = jnp.dot(res_p[:, 2048:2112], dkv_ref[...], preferred_element_type=F32)
    for r in range(4):
        res_o = res_o + jnp.where(col_req == r, part[:, r * HD : (r + 1) * HD], 0.0)

    for key in order:
        t, half, way = key
        if t > 0:
            ring[t - 1, half, way].wait_recv()
            ring[key].start()
    for key in order:
        t, half, way = key
        if t == 3 or (t == 2 and half != way):
            ring[key].wait_recv()
    for copy in q_copies:
        copy.wait_recv()

    own_pages = pltpu.make_async_copy(pg_out.at[me], pool.at[me], lsem.at[5])
    own_pages.start()

    def page_copy(k):
        to = (me + k) % 64
        return remote(pg_out.at[to], pool.at[me], pg_s.at[k], pg_r.at[k], ctx=to)

    def page_start(k, _):
        page_copy(k).start()
        return 0

    lax.fori_loop(1, 64, page_start, 0)

    def scores(k, head, slot):
        keys = kvbuf[head].reshape(KEYS, HD)
        s_ref[slot] = lax.dot_general(keys, qbuf[k % NR, head], NT, preferred_element_type=F32)

    def attend(k, head, slot):
        at_q = z * NR + (rest + 2 * NR - k) % NR
        q_pos = blocks_ref[at_q]
        hide = []
        peak = None
        for d in range(NZ):
            k_pos = blocks_ref[((z + d) % NZ) * NR + rest]
            hide.append(jnp.minimum(q_pos - k_pos, 0).astype(F32) * -NEG)
            first = d * 2 * TOK
            top = fold8(s_ref[slot, first : first + TOK, :])
            peak = top if peak is None else jnp.maximum(peak, top)
            if d == 0:
                s_ref[slot, TOK : 2 * TOK, :] = s_ref[slot, TOK : 2 * TOK, :] + dbias[...]
            top = fold8(s_ref[slot, first + TOK : first + 2 * TOK, :])
            peak = jnp.maximum(peak, top + hide[d])
        m = jnp.max(peak, axis=0, keepdims=True) * score_c
        weights = []
        values = []
        for d in range(NZ):
            first = d * 2 * TOK
            weights.append(jnp.exp2(s_ref[slot, first : first + TOK, :] * score_c - m).astype(BF16))
            shift = m - hide[d]
            weights.append(
                jnp.exp2(s_ref[slot, first + TOK : first + 2 * TOK, :] * score_c - shift).astype(BF16)
            )
            values.append(kvbuf[2 + head, d, 0])
            values.append(kvbuf[2 + head, d, 1])
        values = jnp.concatenate(values, axis=1)
        values = jnp.concatenate([values, jnp.ones((16, KEYS), BF16)], axis=0)
        o = jnp.dot(values, jnp.concatenate(weights, axis=0), preferred_element_type=F32)
        total = o[HD : HD + 1]
        obuf[k % NR, head] = (o[:HD] * (1.0 / total)).astype(BF16)
        lse = m + jnp.log2(total)
        for g in range(GROUP):
            stbuf[k % NR, head * GROUP + g : head * GROUP + g + 1, :] = lse[:, g * TOK : (g + 1) * TOK]

    def o_copy(k):
        to = z * NR + (rest + 2 * NR - k) % NR
        return remote(obuf.at[k], orecv.at[k], o_s.at[k], o_r.at[k], ctx=to)

    def st_copy(k):
        to = z * NR + (rest + 2 * NR - k) % NR
        return remote(stbuf.at[k], strecv.at[k], st_s.at[k], st_r.at[k], ctx=to)

    dbias[...] = jnp.zeros_like(dbias)
    scores(1, 0, 0)

    def step(k, _):
        @pl.when(k == NR)
        def _():
            key_at = lax.broadcasted_iota(jnp.int32, (TOK, QROWS), 0)
            query_at = lax.broadcasted_iota(jnp.int32, (TOK, QROWS), 1) % TOK
            dbias[...] = jnp.where(key_at <= query_at, 0.0, NEG)

        scores(k, 1, 1)
        attend(k, 0, 0)
        scores(k + 1, 0, 0)
        attend(k, 1, 1)

        @pl.when(k < NR)
        def _():
            o_copy(k).start()
            st_copy(k).start()

        return 0

    lax.fori_loop(1, NR + 1, step, 0)

    def page_wait(k, _):
        source = (me + 64 - k) % 64
        to = (me + k) % 64
        remote(pg_out.at[to], pool.at[source], pg_s.at[k], pg_r.at[k], ctx=to).wait()
        return 0

    lax.fori_loop(1, 64, page_wait, 0)
    own_pages.wait()
    pool_rows = pool[...].reshape(POOL, HD)
    found = lax.dot_general(dq, pool_rows, NT, preferred_element_type=F32)
    at = lax.broadcasted_iota(jnp.int32, (1, POOL), 1)
    found = jnp.where((owner_ref[...] == col_req) & (at % 4 == col_head * 2), found, NEG)
    pool_m, pool_l, pool_p = weigh(found)
    pool_o = jnp.dot(pool_p, pool_rows, preferred_element_type=F32)
    both = jnp.maximum(res_m, pool_m)
    res_a = jnp.exp2(res_m - both)
    pool_a = jnp.exp2(pool_m - both)
    dec = (res_o * res_a + pool_o * pool_a) / (res_l * res_a + pool_l * pool_a)
    for h in range(8):
        lhs[TOK : TOK + 16, h * HD : (h + 1) * HD] = dec[h * 16 : (h + 1) * 16, :].astype(BF16)

    for k in range(1, NR):
        remote(
            obuf.at[k], orecv.at[k], o_s.at[k], o_r.at[k], ctx=z * NR + (rest + NR - k) % NR
        ).wait()
        remote(
            stbuf.at[k], strecv.at[k], st_s.at[k], st_r.at[k], ctx=z * NR + (rest + NR - k) % NR
        ).wait()
    lse = [stbuf[0]] + [strecv[k] for k in range(1, NR)]
    top = functools.reduce(jnp.maximum, lse)
    share = [jnp.exp2(x - top) for x in lse]
    whole = 1.0 / functools.reduce(jnp.add, share)
    share = [x * whole for x in share]
    for h in range(8):
        head, g = h // GROUP, h % GROUP
        cols = slice(g * TOK, (g + 1) * TOK)
        merged = obuf[0, head, :, cols].astype(F32) * share[0][h : h + 1]
        for k in range(1, NR):
            merged = merged + orecv[k, head, :, cols].astype(F32) * share[k][h : h + 1]
        lhs[:TOK, h * HD : (h + 1) * HD] = merged.T.astype(BF16)

    core = tp % 2
    side = tp // 2
    sibling = side * 2 + (1 - core)
    across = (1 - side) * 2 + core
    local[4].wait()

    def first_copy(c):
        if c == CHUNKS:
            return remote(pdec.at[:, 1 - core], rdec, t1_s.at[c], t1_r.at[c], tp=sibling)
        return remote(pbuf.at[c, :, 1 - core], rbuf.at[c], t1_s.at[c], t1_r.at[c], tp=sibling)

    def second_copy(c):
        if c == CHUNKS:
            return remote(sdec, tdec, t2_s.at[c], t2_r.at[c], tp=across)
        return remote(sbuf.at[c], tbuf.at[c], t2_s.at[c], t2_r.at[c], tp=across)

    def second(c):
        first_copy(c).wait_recv()
        if c == CHUNKS:
            sdec[...] = (
                pdec[1 - side, core].astype(F32) + rdec[1 - side].astype(F32)
            ).astype(BF16)
        else:
            sbuf[c] = (
                pbuf[c, 1 - side, core].astype(F32) + rbuf[c, 1 - side].astype(F32)
            ).astype(BF16)
        second_copy(c).start()

    dec_parts = []
    for c in range(CHUNKS):
        part = jnp.dot(lhs[...], wbuf[:, c * COLS : (c + 1) * COLS], preferred_element_type=F32)
        pbuf[c] = part[:TOK].astype(BF16).reshape(2, 2, TOK // 4, COLS)
        dec_parts.append(part[TOK:])
        first_copy(c).start()
        if c > 0:
            second(c - 1)
    for t in range(4):
        rows = jnp.concatenate([part[t * 4 : (t + 1) * 4] for part in dec_parts], axis=0)
        pdec[t // 2, t % 2] = rows.astype(BF16)
    first_copy(CHUNKS).start()
    second(CHUNKS - 1)
    second(CHUNKS)
    for c in range(CHUNKS):
        second_copy(c).wait_recv()
        out_ref[:, c * COLS : (c + 1) * COLS] = (
            pbuf[c, side, core].astype(F32) + rbuf[c, side].astype(F32) + tbuf[c].astype(F32)
        ).astype(BF16)
    second_copy(CHUNKS).wait_recv()
    rows = pdec[side, core].astype(F32) + rdec[side].astype(F32) + tdec[...].astype(F32)
    dout_ref[...] = jnp.concatenate(
        [rows[c * 4 : (c + 1) * 4] for c in range(CHUNKS)], axis=1
    ).astype(BF16)

    for key in order:
        ring[key].wait_send()
    for copy in q_copies:
        copy.wait_send()
    for c in range(CHUNKS + 1):
        first_copy(c).wait_send()
        second_copy(c).wait_send()


def body(
    span_q, cache_kv, span_kv, span_blocks, parked_pages, page_dest, page_req,
    decode_cache, decode_lengths, decode_q, decode_kv, out_weight,
):
    me = lax.axis_index("ctx")
    q = span_q.reshape(TOK, 2, GROUP, HD).transpose(1, 2, 0, 3).reshape(2, QROWS, HD)
    kv = jnp.stack([cache_kv, span_kv], axis=0)
    keys = kv[:, :, :, 0].transpose(2, 0, 1, 3)
    values = kv[:, :, :, 1].transpose(2, 0, 3, 1)
    kv = jnp.concatenate([keys, values], axis=0)
    pages = parked_pages.reshape(64, PAGE_ROWS, HD)

    targets = page_dest[:, 0].reshape(64, 64)
    own = lax.dynamic_index_in_dim(targets, me, 0, keepdims=False)
    slot = jnp.arange(64, dtype=jnp.int32)
    hit = own[None, :] == slot[:, None]
    first = jnp.min(jnp.where(hit, slot[None, :], 63), axis=1)
    last = jnp.max(jnp.where(hit, slot[None, :], 0), axis=1)
    page_ix = jnp.stack([first, last], axis=1).reshape(128)
    code = slot[None, :] * 4 + page_req.reshape(64, 64)
    here = targets == me
    low = jnp.min(jnp.where(here, code, 1 << 20), axis=1)
    high = jnp.max(jnp.where(here, code, -1), axis=1)
    owner = jnp.stack(
        [jnp.where(high >= 0, low % 4, -1), jnp.where(high > low, high % 4, -1)], axis=1
    )
    owner = jnp.broadcast_to(owner[:, :, None], (64, 2, PAGE_ROWS)).reshape(1, POOL)

    smem = pl.BlockSpec(memory_space=pltpu.SMEM)
    vmem = pl.BlockSpec(memory_space=pltpu.VMEM)
    hbm = pl.BlockSpec(memory_space=pl.ANY)
    dma = pltpu.SemaphoreType.DMA
    out, dout = pl.pallas_call(
        kernel,
        name="layer",
        out_shape=[
            jax.ShapeDtypeStruct((TOK // 4, CHUNKS * COLS), BF16),
            jax.ShapeDtypeStruct((4, CHUNKS * COLS), BF16),
        ],
        in_specs=[smem, smem, smem, hbm, hbm, hbm, vmem, hbm, vmem, vmem, hbm],
        out_specs=[vmem, vmem],
        scratch_shapes=[
            pltpu.VMEM((4, NZ, 2, HD, HD), BF16),
            pltpu.VMEM((NR, 2, QROWS, HD), BF16),
            pltpu.VMEM((2, KEYS, QROWS), F32),
            pltpu.VMEM((NR, 2, HD, QROWS), BF16),
            pltpu.VMEM((NR, 2, HD, QROWS), BF16),
            pltpu.VMEM((NR, 8, TOK), F32),
            pltpu.VMEM((NR, 8, TOK), F32),
            pltpu.VMEM((TOK, QROWS), F32),
            pltpu.VMEM((64, PAGE_ROWS, HD), BF16),
            pltpu.VMEM((64, 2 * PAGE_ROWS, HD), BF16),
            pltpu.VMEM((64, 2 * PAGE_ROWS, HD), BF16),
            pltpu.VMEM((4 * 2048, HD), BF16),
            pltpu.VMEM((8 * HD, CHUNKS * COLS), BF16),
            pltpu.VMEM((TOK + 16, 8 * HD), BF16),
            pltpu.VMEM((CHUNKS, 2, 2, TOK // 4, COLS), BF16),
            pltpu.VMEM((CHUNKS, 2, TOK // 4, COLS), BF16),
            pltpu.VMEM((CHUNKS, TOK // 4, COLS), BF16),
            pltpu.VMEM((CHUNKS, TOK // 4, COLS), BF16),
            pltpu.VMEM((2, 2, 16, COLS), BF16),
            pltpu.VMEM((2, 16, COLS), BF16),
            pltpu.VMEM((16, COLS), BF16),
            pltpu.VMEM((16, COLS), BF16),
            dma((6,)),
            dma((2, 4, 2)), dma((2, 4, 2)),
            dma((NR,)), dma((NR,)),
            dma((NR,)), dma((NR,)),
            dma((NR,)), dma((NR,)),
            dma((64,)), dma((64,)),
            dma((CHUNKS + 1,)), dma((CHUNKS + 1,)),
            dma((CHUNKS + 1,)), dma((CHUNKS + 1,)),
        ],
        compiler_params=pltpu.CompilerParams(
            collective_id=0, has_side_effects=True, vmem_limit_bytes=56 << 20
        ),
    )(
        span_blocks, page_ix, decode_lengths, q, kv, pages, owner,
        decode_cache.reshape(4 * 2048, HD), decode_q.reshape(128, HD), decode_kv.reshape(64, HD),
        out_weight.reshape(8 * HD, CHUNKS * COLS),
    )
    return out, dout.reshape(1, 4, CHUNKS * COLS)


def solution(mesh):
    return jax.shard_map(
        body,
        mesh=mesh,
        in_specs=(
            P("ctx", "tp", None),
            P("ctx", "tp", None, None),
            P("ctx", "tp", None, None),
            P(),
            P("ctx", None, "tp", None, None),
            P(),
            P(),
            P("ctx", None, "tp", None, None),
            P("ctx"),
            P("ctx", None, "tp", None),
            P("ctx", None, "tp", None, None),
            P("tp", None, None),
        ),
        out_specs=(P(("ctx", "tp"), None), P(("ctx", "tp"), None, None)),
        check_vma=False,
    )
```

time: 404 us -> 114 us (0.28)
  waiting for transfers between devices: 192 us -> 0 us
  Pallas kernels: 0 us -> 100 us
  matrix products: 70.4 us -> 0 us
  other arithmetic: 58.3 us -> 2.41 us
  local copies, waits for them, and re-layouts: 48.1 us -> 10.1 us
  starting transfers between devices: 15.7 us -> 0 us
  between operations: 16.4 us -> 0.71 us
    all_gather x2 -> x0, waiting for transfers between devices: 154 us -> none  [the longest x1 78.7 us: body(): lax.all_gather(cache_kv, 'ctx', axis=0, tiled=True)]
    pallas_call x0 -> x1, Pallas kernels: none -> 100 us  [body(): pl.pallas_call(kernel, name='layer', out_shape=[jax.ShapeDtypeStruct((TOK...]
    dot_general x41 -> x0, matrix products: 70.4 us -> none  [the longest x16 27.2 us: attend_tile(): jnp.einsum('tkgd,nkd->kgtn', grouped_q, key_rows, preferred_element_type=...]
    reduce_sum x29 -> x0, other arithmetic: 41.2 us -> none  [the longest x16 34.7 us: attend_tile(): denominator = denominator * shrink + jnp.sum(weights, axis=-1)]
    squeeze x16 -> x0, local copies, waits for them, and re-layouts: 21.1 us -> none  [make_fold(): result, _ = lax.scan(scan_step, softmax_state, (tiles, tile_starts))]
    reduce_scatter x1 -> x0, waiting for transfers between devices: 19.8 us -> none  [body(): lax.psum_scatter(jnp.dot(flat_attn, weight, preferred_element_type=jnp.fl...]
    all_to_all x1 -> x0, waiting for transfers between devices: 18.6 us -> none  [body(): lax.all_to_all(outgoing.reshape(ctx_count, slot_depth, page_width), 'ctx'...]
    all_to_all x1 -> x0, starting transfers between devices: 15.4 us -> none  [body(): lax.all_to_all(outgoing.reshape(ctx_count, slot_depth, page_width), 'ctx'...]
  transfers between devices with their start and end apart: 5 -> 0, of which waited for: 4 -> 0; matrix products, arithmetic and copies ran while one was open for 43% -> 0% of each run, Pallas kernels for 0% -> 0%
where the time goes in v1:
time: 114 us
  Pallas kernels  100 us (88%)
  local copies, waits for them, and re-layouts  10.1 us (9%)
  other arithmetic  2.41 us (2%)
    pallas_call x1, Pallas kernels, body(): pl.pallas_call(kernel, name='layer', out_shape=[jax.ShapeDtypeStruct((TOK...  100 us
    unnamed x5, local copies, waits for them, and re-layouts  5.63 us

profile of v1, /device:TPU:1, one launch (start us, length us, event | category | flops | bytes accessed | tf_op | source)
XLA Modules:
  0.0 113.6 jit_solution(16665350335849669758)
XLA Ops:
  0.6 0.5 broadcast.137
  1.2 1.4 %reduce.3 = s32[4096]{0:T(1024)S(1)} reduce(s32[4096,1]{0,1:T(1,128)} %param.17, s32[]{:T(128)} %broadcast.137), dimensions={1}, to_apply=%param.17.reduce_sub_computation.3 | reduce | bytes 32772 | tf_op args[5]
  2.6 0.1 reshape_squeeze.3
  2.6 0.1 select_reduce_fusion.3
  2.8 0.1 copy.26
  2.9 0.7 reshape.153.page_ix_ref
  3.6 0.8 reshape.157
  4.4 0.1 select_reduce_fusion.1
  4.5 0.1 copy.31
  4.6 0.1 broadcast_in_dim.50
  4.8 0.7 reshape.158.owner_ref
  5.5 1.0 copy.28
  6.5 1.0 copy.29
  7.6 0.1 copy.30
  7.7 0.7 pad_maximum_fusion.kv_in
  8.5 1.7 %copy.27 = bf16[128,2,4,128]{3,0,2,1:T(8,128)(2,1)} copy(bf16[128,2,4,128]{3,2,1,0:T(4,128)(2,1)} %bitcast.37) | data formatting | bytes 524288 | tf_op jit(solution)/shard_map/reshape | solution.py:352
  10.1 100.4 %layer.1 = (bf16[32,4096]{1,0:T(8,128)(2,1)}, bf16[4,4096]{1,0:T(4,128)(2,1)}) custom-call(s32[64]{0:T(128)} %blocks_ref.1, s32[128]{0:T(128)} %reshape.153.page_ix_ref, s32[4]{0:T(128)} %lens_ref.1, bf16[2,512,128]{2,1,0:T(8,128)(2,1)} %bitcast.33, bf16[4,2,128,128]{3,2,1,0:T(8,128)(2,1)} %pad_maximum_fusion.kv_in, bf16[64,32,128]{2,1,0:T(8,128)(2,1)} %bitcast.34, ...), custom_call_target="tpu_custom_call" | custom-call | tf_op jit(solution)/shard_map/layer/pallas_call | solution.py:379
  110.5 1.7 %copy.34 = bf16[32,4096]{1,0:T(8,128)(2,1)} copy(bf16[32,4096]{1,0:T(8,128)(2,1)} %get-tuple-element.16) | data formatting | bytes 524288
  112.2 1.4 %copy.35 = bf16[1,4,4096]{2,1,0:T(4,128)(2,1)} copy(bf16[1,4,4096]{2,1,0:T(4,128)(2,1)} %bitcast.39) | data formatting | bytes 65536
  (6 shorter events, 0.1 us)

commit v2 on v1

v2 whole, which is shorter than its diff:
```python
import functools

import jax
import jax.numpy as jnp
from jax import lax
from jax.experimental import pallas as pl
from jax.experimental.pallas import tpu as pltpu
from jax.sharding import PartitionSpec as P

NEG = -1e30
LOG2E = 1.4426950408889634
MESH = pl.DeviceIdType.MESH
BF16 = jnp.bfloat16
F32 = jnp.float32
NT = (((1,), (1,)), ((), ()))

NZ, NR = 8, 8
TOK = 128
HD = 128
GROUP = 4
QROWS = GROUP * TOK
PHASES = ((0, 1, 7), (2, 6, 3, 5, 4))
MOST_KEYS = 5 * 2 * TOK
DX = (0, 0, 1, 3, 2, 1, 3, 2)
DY = (0, 1, 0, 0, 0, 1, 1, 1)
COLS = 1024
CHUNKS = 4
PAGE_ROWS = 32
POOL = 4096


def remote(src, dst, send, recv, **device):
    return pltpu.make_async_remote_copy(
        src_ref=src, dst_ref=dst, send_sem=send, recv_sem=recv, device_id=device, device_id_type=MESH
    )


def fold8(x):
    return jnp.max(x.reshape(x.shape[0] // 8, 8, x.shape[1]), axis=0)


def kernel(
    blocks_ref, lens_ref, q_in, cache_in, span_in, pages_in, dest_in, req_in, dcache_in, dq_in, dkv_in, w_in,
    out_ref, dout_ref,
    q_raw, kv_raw, dest, req, dq_raw, dkv, page_ix, page_at, hide,
    kvbuf, qbuf, s_ref, acc, peaks, obuf, orecv, stbuf, strecv, pages, pg_out, pool, dcache, wbuf,
    lhs, pbuf, rbuf, sbuf, tbuf, pdec, rdec, sdec, tdec,
    lsem, kv_s, kv_r, q_s, q_r, o_s, o_r, st_s, st_r, pg_s, pg_r, t1_s, t1_r, t2_s, t2_r,
):
    me = lax.axis_index("ctx")
    tp = lax.axis_index("tp")
    z = me // NR
    rest = me % NR
    y = rest // 4
    x = rest % 4
    score_c = (HD ** -0.5) * LOG2E

    def plane(dx, dy):
        return z * NR + ((y + dy) % 2) * 4 + (x + dx) % 4

    barrier = pltpu.get_barrier_semaphore()

    def greet(k, _):
        pl.semaphore_signal(barrier, inc=1, device_id={"ctx": (me + k) % 64}, device_id_type=MESH)
        return 0

    lax.fori_loop(1, 64, greet, 0)
    for k in range(1, 4):
        pl.semaphore_signal(barrier, inc=1, device_id={"tp": (tp + k) % 4}, device_id_type=MESH)

    moves = [
        (q_in, q_raw), (cache_in, kv_raw.at[0]), (span_in, kv_raw.at[1]), (dest_in, dest), (req_in, req),
        (pages_in, pages), (dq_in, dq_raw), (dkv_in, dkv), (dcache_in, dcache), (w_in, wbuf),
    ]
    local = [pltpu.make_async_copy(src, dst, lsem.at[i]) for i, (src, dst) in enumerate(moves)]
    for copy in local:
        copy.start()

    for k in range(NR):
        q_pos = blocks_ref[plane(4 - DX[k], DY[k])]
        for d in range(NZ):
            k_pos = blocks_ref[((z + d) % NZ) * NR + rest]
            hide[k * NZ + d] = jnp.minimum(q_pos - k_pos, 0).astype(F32) * -NEG

    row = lax.broadcasted_iota(jnp.int32, (128, 128), 0)
    lane = lax.broadcasted_iota(jnp.int32, (128, 128), 1)
    by_head = (lane == (row % 16) * 8 + row // 16).astype(BF16)
    by_kind = (lane == (row % 32) * 4 + row // 32).astype(BF16)
    local[0].wait()
    for b in range(8):
        part = jnp.dot(by_head, q_raw[b * 128 : (b + 1) * 128, :], preferred_element_type=F32)
        for h in range(8):
            at = (h % GROUP) * TOK + b * 16
            qbuf[0, h // GROUP, at : at + 16, :] = part[h * 16 : (h + 1) * 16].astype(BF16)
    local[1].wait()
    local[2].wait()
    for half in range(2):
        parts = [
            jnp.dot(by_kind, kv_raw[half, b * 128 : (b + 1) * 128, :], preferred_element_type=F32)
            for b in range(4)
        ]
        for h in range(2):
            first = h * 64
            keys = jnp.concatenate([part[first : first + 32] for part in parts], axis=0)
            values = jnp.concatenate([part[first + 32 : first + 64] for part in parts], axis=0)
            kvbuf[h, 0, half] = keys.astype(BF16)
            kvbuf[2 + h, 0, half] = values.T.astype(BF16)

    local[3].wait()
    own_row = dest[pl.ds(me // 2, 1), :]
    slot_lane = lax.broadcasted_iota(jnp.int32, (64, 128), 1)
    hit = (own_row == lax.broadcasted_iota(jnp.int32, (64, 128), 0)) & (slot_lane // 64 == me % 2)
    first = jnp.min(jnp.where(hit, slot_lane % 64, 63), axis=1, keepdims=True)
    last = jnp.max(jnp.where(hit, slot_lane % 64, 0), axis=1, keepdims=True)
    page_ix[...] = jnp.where(slot_lane < 64, first, last)
    to_smem = pltpu.make_async_copy(page_ix, page_at, lsem.at[10])
    to_smem.start()

    local[4].wait()
    code_lane = lax.broadcasted_iota(jnp.int32, (32, 128), 1)
    code = (code_lane % 64) * 4 + req[...]
    owners = [None] * 4
    for odd in range(2):
        hit = (dest[...] == me) & (code_lane // 64 == odd)
        low = jnp.min(jnp.where(hit, code, 1 << 20), axis=1, keepdims=True)
        high = jnp.max(jnp.where(hit, code, -1), axis=1, keepdims=True)
        owners[odd] = jnp.where(high >= 0, low % 4, -1)
        owners[2 + odd] = jnp.where(high > low, high % 4, -1)
    owner = jnp.concatenate(owners, axis=0)
    owned = (owner == (lane // 4) % 4).astype(BF16)
    to_smem.wait()

    pl.semaphore_wait(barrier, 66)

    def q_copy(k, head):
        if k < 5:
            src, to = 0, plane(DX[k], DY[k])
        elif head == 0:
            src, to = 1, plane(DX[k], 0)
        else:
            src, to = k - 3, plane(0, 1)
        return remote(qbuf.at[src, head], qbuf.at[k, head], q_s.at[k, head], q_r.at[k, head], ctx=to)

    def ring(t, half, way):
        here = (-t) % NZ if way == 0 else t
        there = (-t - 1) % NZ if way == 0 else t + 1
        to = (z + 1) % NZ if way == 0 else (z + NZ - 1) % NZ
        return remote(
            kvbuf.at[:, here, half], kvbuf.at[:, there, half],
            kv_s.at[way, t, half], kv_r.at[way, t, half], ctx=to * NR + rest,
        )

    def ring_step(t, half):
        for way in range(2):
            if t < 3 or half == way:
                if t > 0:
                    ring(t - 1, half, way).wait_recv()
                ring(t, half, way).start()

    q_copy(1, 0).start()
    ring_step(0, 0)
    for k in (2, 3, 4):
        q_copy(k, 1).start()
    ring_step(0, 1)
    for k in (2, 3, 4):
        q_copy(k, 0).start()
    q_copy(1, 1).start()

    local[5].wait()

    def place(t, _):
        for i in range(2):
            pg_out[t, i * PAGE_ROWS : (i + 1) * PAGE_ROWS, :] = pages[page_at[t, i * 64]]
        return 0

    lax.fori_loop(0, 64, place, 0)
    own_pages = pltpu.make_async_copy(pg_out.at[me], pool.at[me], lsem.at[11])
    own_pages.start()

    ring_step(1, 0)

    local[6].wait()
    local[7].wait()
    local[8].wait()
    dq = jnp.dot(by_head, dq_raw[...], preferred_element_type=F32).astype(BF16)
    col_req = (lax.broadcasted_iota(jnp.int32, (128, 1), 0) // 4) % 4
    col_step = lax.broadcasted_iota(jnp.int32, (128, 1), 0) % 4
    col_head = lax.broadcasted_iota(jnp.int32, (128, 1), 0) // 64
    length = jnp.zeros((128, 1), jnp.int32)
    for r in range(4):
        length = jnp.where(col_req == r, lens_ref[r], length)

    def weigh(scores):
        m = jnp.max(scores, axis=1, keepdims=True)
        p = jnp.exp2(scores * score_c - m * score_c)
        total = jnp.sum(p, axis=1, keepdims=True)
        return m * score_c, total, pltpu.roll(p, 1, 1).astype(BF16)

    wide = jnp.concatenate([dcache[r * 2048 : (r + 1) * 2048, :] for r in range(4)], axis=1)
    zero = jnp.zeros((), BF16)
    dq_wide = jnp.concatenate([jnp.where(col_req == r, dq, zero) for r in range(4)], axis=1)
    res = lax.dot_general(dq_wide, wide, NT, preferred_element_type=F32)
    at = lax.broadcasted_iota(jnp.int32, (1, 2048), 1)
    res = jnp.where((at // 4 < length) & (at % 4 == col_head * 2), res, NEG)
    new = lax.dot_general(dq, dkv[...], NT, preferred_element_type=F32)
    at = lax.broadcasted_iota(jnp.int32, (1, 64), 1)
    new = jnp.where(
        (at // 16 == col_req) & ((at // 4) % 4 <= col_step) & (at % 4 == col_head * 2), new, NEG
    )
    new = jnp.concatenate([new, jnp.full((128, 64), NEG, F32)], axis=1)
    res_m, res_l, res_p = weigh(jnp.concatenate([res, new], axis=1))
    part = jnp.dot(res_p[:, :2048], wide, preferred_element_type=F32)
    res_o = jnp.dot(res_p[:, 2048:2112], dkv[...], preferred_element_type=F32)
    for r in range(4):
        res_o = res_o + jnp.where(col_req == r, part[:, r * HD : (r + 1) * HD], 0.0)

    q_copy(1, 0).wait_recv()
    for k in (5, 6, 7):
        q_copy(k, 0).start()
    ring_step(1, 1)

    def scores(phase, k, head, slot):
        keys = jnp.concatenate([kvbuf[head, d].reshape(2 * TOK, HD) for d in PHASES[phase]], axis=0)
        s_ref[slot, : len(PHASES[phase]) * 2 * TOK, :] = lax.dot_general(
            keys, qbuf[k, head], NT, preferred_element_type=F32
        )

    def attend(phase, k, head, slot, own=False):
        peak = None if phase == 0 else peaks[k, head]
        shifts = []
        for i, d in enumerate(PHASES[phase]):
            cached = slice(i * 2 * TOK, (i * 2 + 1) * TOK)
            fresh = slice((i * 2 + 1) * TOK, (i * 2 + 2) * TOK)
            shifts.append(hide[k * NZ + d])
            top = fold8(s_ref[slot, cached, :])
            peak = top if peak is None else jnp.maximum(peak, top)
            if own and d == 0:
                key_at = lax.broadcasted_iota(jnp.int32, (TOK, QROWS), 0)
                query_at = lax.broadcasted_iota(jnp.int32, (TOK, QROWS), 1) % TOK
                s_ref[slot, fresh, :] = jnp.where(key_at <= query_at, s_ref[slot, fresh, :], NEG)
            peak = jnp.maximum(peak, fold8(s_ref[slot, fresh, :]) + shifts[-1])
        m = jnp.max(peak, axis=0, keepdims=True) * score_c
        weights = []
        values = []
        for i, d in enumerate(PHASES[phase]):
            cached = slice(i * 2 * TOK, (i * 2 + 1) * TOK)
            fresh = slice((i * 2 + 1) * TOK, (i * 2 + 2) * TOK)
            weights.append(jnp.exp2(s_ref[slot, cached, :] * score_c - m).astype(BF16))
            weights.append(jnp.exp2(s_ref[slot, fresh, :] * score_c - (m - shifts[i])).astype(BF16))
            values.append(kvbuf[2 + head, d, 0])
            values.append(kvbuf[2 + head, d, 1])
        values = jnp.concatenate(values, axis=1)
        values = jnp.concatenate([values, jnp.ones((16, values.shape[1]), BF16)], axis=0)
        o = jnp.dot(values, jnp.concatenate(weights, axis=0), preferred_element_type=F32)[: HD + 8]
        if phase == 0:
            acc[k, head] = o
            peaks[k, head] = peak
            return
        before = jnp.max(peaks[k, head], axis=0, keepdims=True) * score_c
        o = o + acc[k, head] * jnp.exp2(before - m)
        total = o[HD : HD + 1]
        obuf[k, head] = (o[:HD] * (1.0 / total)).astype(BF16)
        lse = m + jnp.log2(total)
        for g in range(GROUP):
            stbuf[k, head * GROUP + g : head * GROUP + g + 1, :] = lse[:, g * TOK : (g + 1) * TOK]

    def o_copy(k):
        return remote(obuf.at[k], orecv.at[k], o_s.at[k], o_r.at[k], ctx=plane(4 - DX[k], DY[k]))

    def st_copy(k):
        return remote(stbuf.at[k], strecv.at[k], st_s.at[k], st_r.at[k], ctx=plane(4 - DX[k], DY[k]))

    def step0(k, own=False):
        scores(0, k, 1, 1)
        attend(0, k, 0, 0, own)
        scores(0, (k + 1) % NR, 0, 0)
        attend(0, k, 1, 1, own)

    scores(0, 0, 0, 0)
    q_copy(1, 1).wait_recv()
    step0(0, True)

    def first_phase(k, _):
        @pl.when(k == 1)
        def _():
            q_copy(2, 0).wait_recv()
            q_copy(2, 1).wait_recv()
            q_copy(5, 1).start()

        @pl.when(k == 2)
        def _():
            ring_step(2, 0)
            for i in (3, 4):
                q_copy(i, 1).wait_recv()
                q_copy(i + 3, 1).start()
            q_copy(3, 0).wait_recv()

        @pl.when(k == 3)
        def _():
            q_copy(4, 0).wait_recv()

        @pl.when(k == 4)
        def _():
            ring_step(2, 1)

        for i in (4, 5, 6):
            @pl.when(k == i)
            def _():
                q_copy(i + 1, 0).wait_recv()
                q_copy(i + 1, 1).wait_recv()

        step0(k)
        return 0

    lax.fori_loop(1, NR, first_phase, 0)
    ring_step(3, 0)
    ring_step(3, 1)

    def page_copy(k):
        to = (me + k) % 64
        return remote(pg_out.at[to], pool.at[me], pg_s.at[k], pg_r.at[k], ctx=to)

    def page_start(k, _):
        page_copy(k).start()
        return 0

    lax.fori_loop(1, 64, page_start, 0)

    for t, half, way in ((2, 1, 0), (2, 0, 1), (3, 0, 0), (3, 1, 1)):
        ring(t, half, way).wait_recv()

    scores(1, 1, 0, 0)

    def second_phase(j, _):
        k = j % NR
        scores(1, k, 1, 1)
        attend(1, k, 0, 0)
        scores(1, (j + 1) % NR, 0, 0)
        attend(1, k, 1, 1)
        for i in range(1, NR):
            @pl.when(j == i)
            def _():
                o_copy(i).start()
                st_copy(i).start()

        return 0

    lax.fori_loop(1, NR + 1, second_phase, 0)

    def page_wait(k, _):
        source = (me + 64 - k) % 64
        to = (me + k) % 64
        remote(pg_out.at[to], pool.at[source], pg_s.at[k], pg_r.at[k], ctx=to).wait()
        return 0

    lax.fori_loop(1, 64, page_wait, 0)
    own_pages.wait()
    pool_rows = pool[...].reshape(POOL, HD)
    found = lax.dot_general(dq, pool_rows, NT, preferred_element_type=F32)
    at = lax.broadcasted_iota(jnp.int32, (128, POOL), 1)
    slot_at = (at // 32) % 2 * 64 + (at // 64) % 2 * 32 + at // 128
    spread = (lax.broadcasted_iota(jnp.int32, (128, POOL), 0) == slot_at).astype(BF16)
    mine = lax.dot_general(owned, spread, (((0,), (0,)), ((), ())), preferred_element_type=F32)
    at = lax.broadcasted_iota(jnp.int32, (1, POOL), 1)
    found = jnp.where((mine > 0.5) & (at % 4 == col_head * 2), found, NEG)
    pool_m, pool_l, pool_p = weigh(found)
    pool_o = jnp.dot(pool_p, pool_rows, preferred_element_type=F32)
    both = jnp.maximum(res_m, pool_m)
    res_a = jnp.exp2(res_m - both)
    pool_a = jnp.exp2(pool_m - both)
    dec = (res_o * res_a + pool_o * pool_a) / (res_l * res_a + pool_l * pool_a)
    for h in range(8):
        lhs[TOK : TOK + 16, h * HD : (h + 1) * HD] = dec[h * 16 : (h + 1) * 16, :].astype(BF16)

    for k in range(1, NR):
        o_copy(k).wait()
        st_copy(k).wait()
    lse = [stbuf[0]] + [strecv[k] for k in range(1, NR)]
    top = functools.reduce(jnp.maximum, lse)
    share = [jnp.exp2(a - top) for a in lse]
    whole = 1.0 / functools.reduce(jnp.add, share)
    share = [a * whole for a in share]
    for h in range(8):
        head, g = h // GROUP, h % GROUP
        cols = slice(g * TOK, (g + 1) * TOK)
        merged = obuf[0, head, :, cols].astype(F32) * share[0][h : h + 1]
        for k in range(1, NR):
            merged = merged + orecv[k, head, :, cols].astype(F32) * share[k][h : h + 1]
        lhs[:TOK, h * HD : (h + 1) * HD] = merged.T.astype(BF16)

    core = tp % 2
    side = tp // 2
    sibling = side * 2 + (1 - core)
    across = (1 - side) * 2 + core
    local[9].wait()

    def first_copy(c):
        if c == CHUNKS:
            return remote(pdec.at[:, 1 - core], rdec, t1_s.at[c], t1_r.at[c], tp=sibling)
        return remote(pbuf.at[c, :, 1 - core], rbuf.at[c], t1_s.at[c], t1_r.at[c], tp=sibling)

    def second_copy(c):
        if c == CHUNKS:
            return remote(sdec, tdec, t2_s.at[c], t2_r.at[c], tp=across)
        return remote(sbuf.at[c], tbuf.at[c], t2_s.at[c], t2_r.at[c], tp=across)

    def second(c):
        first_copy(c).wait_recv()
        if c == CHUNKS:
            sdec[...] = (
                pdec[1 - side, core].astype(F32) + rdec[1 - side].astype(F32)
            ).astype(BF16)
        else:
            sbuf[c] = (
                pbuf[c, 1 - side, core].astype(F32) + rbuf[c, 1 - side].astype(F32)
            ).astype(BF16)
        second_copy(c).start()

    dec_parts = []
    for c in range(CHUNKS):
        part = jnp.dot(lhs[...], wbuf[:, c * COLS : (c + 1) * COLS], preferred_element_type=F32)
        pbuf[c] = part[:TOK].astype(BF16).reshape(2, 2, TOK // 4, COLS)
        dec_parts.append(part[TOK:])
        first_copy(c).start()
        if c > 0:
            second(c - 1)
    for t in range(4):
        rows = jnp.concatenate([part[t * 4 : (t + 1) * 4] for part in dec_parts], axis=0)
        pdec[t // 2, t % 2] = rows.astype(BF16)
    first_copy(CHUNKS).start()
    second(CHUNKS - 1)
    second(CHUNKS)
    for c in range(CHUNKS):
        second_copy(c).wait_recv()
        out_ref[:, c * COLS : (c + 1) * COLS] = (
            pbuf[c, side, core].astype(F32) + rbuf[c, side].astype(F32) + tbuf[c].astype(F32)
        ).astype(BF16)
    second_copy(CHUNKS).wait_recv()
    rows = pdec[side, core].astype(F32) + rdec[side].astype(F32) + tdec[...].astype(F32)
    dout_ref[...] = jnp.concatenate(
        [rows[c * 4 : (c + 1) * 4] for c in range(CHUNKS)], axis=1
    ).astype(BF16)

    for t in range(4):
        for half in range(2):
            for way in range(2):
                if t < 3 or half == way:
                    ring(t, half, way).wait_send()
    for k in range(1, NR):
        for head in range(2):
            q_copy(k, head).wait_send()
    for c in range(CHUNKS + 1):
        first_copy(c).wait_send()
        second_copy(c).wait_send()


def body(
    span_q, cache_kv, span_kv, span_blocks, parked_pages, page_dest, page_req,
    decode_cache, decode_lengths, decode_q, decode_kv, out_weight,
):
    smem = pl.BlockSpec(memory_space=pltpu.SMEM)
    vmem = pl.BlockSpec(memory_space=pltpu.VMEM)
    hbm = pl.BlockSpec(memory_space=pl.ANY)
    dma = pltpu.SemaphoreType.DMA
    out, dout = pl.pallas_call(
        kernel,
        name="layer",
        out_shape=[
            jax.ShapeDtypeStruct((TOK // 4, CHUNKS * COLS), BF16),
            jax.ShapeDtypeStruct((4, CHUNKS * COLS), BF16),
        ],
        in_specs=[smem] * 2 + [hbm] * 10,
        out_specs=[vmem, vmem],
        scratch_shapes=[
            pltpu.VMEM((8 * TOK, HD), BF16),
            pltpu.VMEM((2, 4 * TOK, HD), BF16),
            pltpu.VMEM((32, 128), jnp.int32),
            pltpu.VMEM((32, 128), jnp.int32),
            pltpu.VMEM((128, HD), BF16),
            pltpu.VMEM((64, HD), BF16),
            pltpu.VMEM((64, 128), jnp.int32),
            pltpu.SMEM((64, 128), jnp.int32),
            pltpu.SMEM((NR * NZ,), F32),
            pltpu.VMEM((4, NZ, 2, HD, HD), BF16),
            pltpu.VMEM((NR, 2, QROWS, HD), BF16),
            pltpu.VMEM((2, MOST_KEYS, QROWS), F32),
            pltpu.VMEM((NR, 2, HD + 8, QROWS), F32),
            pltpu.VMEM((NR, 2, 8, QROWS), F32),
            pltpu.VMEM((NR, 2, HD, QROWS), BF16),
            pltpu.VMEM((NR, 2, HD, QROWS), BF16),
            pltpu.VMEM((NR, 8, TOK), F32),
            pltpu.VMEM((NR, 8, TOK), F32),
            pltpu.VMEM((64, PAGE_ROWS, HD), BF16),
            pltpu.VMEM((64, 2 * PAGE_ROWS, HD), BF16),
            pltpu.VMEM((64, 2 * PAGE_ROWS, HD), BF16),
            pltpu.VMEM((4 * 2048, HD), BF16),
            pltpu.VMEM((8 * HD, CHUNKS * COLS), BF16),
            pltpu.VMEM((TOK + 16, 8 * HD), BF16),
            pltpu.VMEM((CHUNKS, 2, 2, TOK // 4, COLS), BF16),
            pltpu.VMEM((CHUNKS, 2, TOK // 4, COLS), BF16),
            pltpu.VMEM((CHUNKS, TOK // 4, COLS), BF16),
            pltpu.VMEM((CHUNKS, TOK // 4, COLS), BF16),
            pltpu.VMEM((2, 2, 16, COLS), BF16),
            pltpu.VMEM((2, 16, COLS), BF16),
            pltpu.VMEM((16, COLS), BF16),
            pltpu.VMEM((16, COLS), BF16),
            dma((12,)),
            dma((2, 4, 2)), dma((2, 4, 2)),
            dma((NR, 2)), dma((NR, 2)),
            dma((NR,)), dma((NR,)),
            dma((NR,)), dma((NR,)),
            dma((64,)), dma((64,)),
            dma((CHUNKS + 1,)), dma((CHUNKS + 1,)),
            dma((CHUNKS + 1,)), dma((CHUNKS + 1,)),
        ],
        compiler_params=pltpu.CompilerParams(
            collective_id=0, has_side_effects=True, vmem_limit_bytes=56 << 20
        ),
    )(
        span_blocks, decode_lengths, span_q.reshape(8 * TOK, HD),
        cache_kv.reshape(4 * TOK, HD), span_kv.reshape(4 * TOK, HD),
        parked_pages.reshape(64, PAGE_ROWS, HD), page_dest.reshape(32, 128), page_req.reshape(32, 128),
        decode_cache.reshape(4 * 2048, HD), decode_q.reshape(128, HD), decode_kv.reshape(64, HD),
        out_weight.reshape(8 * HD, CHUNKS * COLS),
    )
    return out, dout.reshape(1, 4, CHUNKS * COLS)


def solution(mesh):
    return jax.shard_map(
        body,
        mesh=mesh,
        in_specs=(
            P("ctx", "tp", None),
            P("ctx", "tp", None, None),
            P("ctx", "tp", None, None),
            P(),
            P("ctx", None, "tp", None, None),
            P(),
            P(),
            P("ctx", None, "tp", None, None),
            P("ctx"),
            P("ctx", None, "tp", None),
            P("ctx", None, "tp", None, None),
            P("tp", None, None),
        ),
        out_specs=(P(("ctx", "tp"), None), P(("ctx", "tp"), None, None)),
        check_vma=False,
    )
```

time: 114 us -> 96.7 us (0.85)
  Pallas kernels: 100 us -> 92.8 us
  local copies, waits for them, and re-layouts: 10.1 us -> 3.05 us
  other arithmetic: 2.41 us -> 0 us
    pallas_call x1, Pallas kernels: 100 us -> 92.8 us  [body(): pl.pallas_call(kernel, name='layer', out_shape=[jax.ShapeDtypeStruct((TOK...]
    reshape x4 -> x0, local copies, waits for them, and re-layouts: 3.93 us -> none  [the longest x1 1.69 us: body(): span_q.reshape(TOK, 2, GROUP, HD).transpose(1, 2, 0, 3)]
    unnamed x5 -> x2, local copies, waits for them, and re-layouts: 5.63 us -> 3.05 us
    unnamed x1 -> x0, other arithmetic: 1.4 us -> none
where the time goes in v2:
time: 96.7 us; the launch traced here: 96.5 us
  Pallas kernels  92.8 us (96%)
  local copies, waits for them, and re-layouts  3.05 us (3%)
    pallas_call x1, Pallas kernels, body(): pl.pallas_call(kernel, name='layer', out_shape=[jax.ShapeDtypeStruct((TOK...  92.8 us
    unnamed x2, local copies, waits for them, and re-layouts  3.05 us

profile of v2, /device:TPU:1, one launch (start us, length us, event | category | flops | bytes accessed | tf_op | source)
XLA Modules:
  0.0 96.5 jit_solution(1625721911219392311)
XLA Ops:
  0.6 92.8 %layer.1 = (bf16[32,4096]{1,0:T(8,128)(2,1)}, bf16[4,4096]{1,0:T(4,128)(2,1)}) custom-call(s32[64]{0:T(128)} %blocks_ref.1, s32[4]{0:T(128)} %lens_ref.1, bf16[1024,128]{1,0:T(8,128)(2,1)} %bitcast.14, bf16[512,128]{1,0:T(8,128)(2,1)} %bitcast.15, bf16[512,128]{1,0:T(8,128)(2,1)} %bitcast.16, bf16[64,32,128]{2,1,0:T(8,128)(2,1)} %bitcast.13, ...), custom_call_target="tpu_custom_call" | custom-call | tf_op jit(solution)/shard_map/layer/pallas_call | solution.py:465
  93.4 1.7 %copy.16 = bf16[32,4096]{1,0:T(8,128)(2,1)} copy(bf16[32,4096]{1,0:T(8,128)(2,1)} %get-tuple-element.8) | data formatting | bytes 524288
  95.1 1.4 %copy.17 = bf16[1,4,4096]{2,1,0:T(4,128)(2,1)} copy(bf16[1,4,4096]{2,1,0:T(4,128)(2,1)} %bitcast.18) | data formatting | bytes 65536

commit v3 on v2

--- a/solution.py
+++ b/solution.py
@@ -23,6 +23,7 @@
 MOST_KEYS = 5 * 2 * TOK
 DX = (0, 0, 1, 3, 2, 1, 3, 2)
 DY = (0, 1, 0, 0, 0, 1, 1, 1)
+MESSAGES = 14
 COLS = 1024
 CHUNKS = 4
 PAGE_ROWS = 32
@@ -43,7 +44,7 @@
     blocks_ref, lens_ref, q_in, cache_in, span_in, pages_in, dest_in, req_in, dcache_in, dq_in, dkv_in, w_in,
     out_ref, dout_ref,
     q_raw, kv_raw, dest, req, dq_raw, dkv, page_ix, page_at, hide,
-    kvbuf, qbuf, s_ref, acc, peaks, obuf, orecv, stbuf, strecv, pages, pg_out, pool, dcache, wbuf,
+    kvbuf, qbuf, s_ref, acc, peaks, obuf, orecv, stbuf, strecv, mbuf, mst, pages, pg_out, pool, dcache, wbuf,
     lhs, pbuf, rbuf, sbuf, tbuf, pdec, rdec, sdec, tdec,
     lsem, kv_s, kv_r, q_s, q_r, o_s, o_r, st_s, st_r, pg_s, pg_r, t1_s, t1_r, t2_s, t2_r,
 ):
@@ -261,14 +262,61 @@
         total = o[HD : HD + 1]
         obuf[k, head] = (o[:HD] * (1.0 / total)).astype(BF16)
         lse = m + jnp.log2(total)
-        for g in range(GROUP):
-            stbuf[k, head * GROUP + g : head * GROUP + g + 1, :] = lse[:, g * TOK : (g + 1) * TOK]
-
-    def o_copy(k):
-        return remote(obuf.at[k], orecv.at[k], o_s.at[k], o_r.at[k], ctx=plane(4 - DX[k], DY[k]))
-
-    def st_copy(k):
-        return remote(stbuf.at[k], strecv.at[k], st_s.at[k], st_r.at[k], ctx=plane(4 - DX[k], DY[k]))
+        rows = [lse[:, g * TOK : (g + 1) * TOK] for g in range(GROUP)]
+        stbuf[k, head] = jnp.concatenate(rows + rows, axis=0)
+
+    def messages(i):
+        if i < 4:
+            k = (1, 5, 6, 7)[i]
+            src, stat, to = obuf.at[k, 1], stbuf.at[k, 1], plane(0, 1)
+        elif i < 7:
+            src, stat, to = mbuf.at[i - 4], mst.at[i - 4], plane(4 - DX[i - 2], 0)
+        elif i < 13:
+            src, stat, to = obuf.at[i - 5, 0], stbuf.at[i - 5, 0], plane(4 - DX[i - 5], 0)
+        else:
+            src, stat, to = mbuf.at[3], mst.at[3], plane(0, 1)
+        return [
+            remote(src, orecv.at[i], o_s.at[i], o_r.at[i], ctx=to),
+            remote(stat, strecv.at[i], st_s.at[i], st_r.at[i], ctx=to),
+        ]
+
+    def depart(i):
+        for copy in messages(i):
+            copy.start()
+
+    def arrive(i):
+        for copy in messages(i):
+            copy.wait_recv()
+
+    def merge(parts):
+        stats = [stat[...] for _, stat in parts]
+        top = functools.reduce(jnp.maximum, stats)
+        share = [jnp.exp2(a - top) for a in stats]
+        whole = functools.reduce(jnp.add, share)
+        scale = 1.0 / whole
+        merged = None
+        for (ref, _), a in zip(parts, share):
+            a = a * scale
+            wide = jnp.concatenate([a[g : g + 1] for g in range(GROUP)], axis=1)
+            term = ref[...].astype(F32) * wide
+            merged = term if merged is None else merged + term
+        return merged, top + jnp.log2(whole)
+
+    def mine_of(k, head):
+        return obuf.at[k, head], stbuf.at[k, head]
+
+    def came(i):
+        return orecv.at[i], strecv.at[i]
+
+    def relay(i, parts):
+        merged, stat = merge(parts)
+        mbuf[i] = merged.astype(BF16)
+        mst[i] = stat
+
+    def relay_head1(i):
+        arrive(i - 3)
+        relay(i - 4, [mine_of(i - 2, 1), came(i - 3)])
+        depart(i)
 
     def step0(k, own=False):
         scores(0, k, 1, 1)
@@ -331,21 +379,90 @@
 
     scores(1, 1, 0, 0)
 
+    def second_at(j):
+        t = (j + 1) // 3
+        return (j + 3 * (t % 2) - 3 * (t // 2)) % NR
+
     def second_phase(j, _):
-        k = j % NR
+        k = second_at(j)
         scores(1, k, 1, 1)
         attend(1, k, 0, 0)
-        scores(1, (j + 1) % NR, 0, 0)
+        scores(1, second_at(j + 1), 0, 0)
         attend(1, k, 1, 1)
-        for i in range(1, NR):
+
+        @pl.when(j == 1)
+        def _():
+            depart(0)
+
+        for i in (2, 3, 4):
             @pl.when(j == i)
             def _():
-                o_copy(i).start()
-                st_copy(i).start()
+                depart(i - 1)
+                depart(i + 8)
+
+        for i in (5, 6, 7):
+            @pl.when(j == i)
+            def _():
+                depart(i + 2)
+
+        for i in (6, 7):
+            @pl.when(j == i)
+            def _():
+                relay_head1(i - 2)
 
         return 0
 
     lax.fori_loop(1, NR + 1, second_phase, 0)
+    for i in (10, 11, 12):
+        arrive(i)
+    relay(3, [mine_of(1, 0), came(10), came(11), came(12)])
+    depart(13)
+    relay_head1(6)
+
+    for head in range(2):
+        others = (13, 7, 8, 9) if head == 0 else (0, 4, 5, 6)
+        for i in others:
+            arrive(i)
+        merged, _ = merge([mine_of(0, head)] + [came(i) for i in others])
+        for g in range(GROUP):
+            h = head * GROUP + g
+            lhs[:, h * HD : (h + 1) * HD] = merged[:, g * TOK : (g + 1) * TOK].T.astype(BF16)
+
+    core = tp % 2
+    side = tp // 2
+    sibling = side * 2 + (1 - core)
+    across = (1 - side) * 2 + core
+    local[9].wait()
+
+    def first_copy(c):
+        if c == CHUNKS:
+            return remote(pdec.at[:, 1 - core], rdec, t1_s.at[c], t1_r.at[c], tp=sibling)
+        return remote(pbuf.at[c, :, 1 - core], rbuf.at[c], t1_s.at[c], t1_r.at[c], tp=sibling)
+
+    def second_copy(c):
+        if c == CHUNKS:
+            return remote(sdec, tdec, t2_s.at[c], t2_r.at[c], tp=across)
+        return remote(sbuf.at[c], tbuf.at[c], t2_s.at[c], t2_r.at[c], tp=across)
+
+    def second(c):
+        first_copy(c).wait_recv()
+        if c == CHUNKS:
+            sdec[...] = (
+                pdec[1 - side, core].astype(F32) + rdec[1 - side].astype(F32)
+            ).astype(BF16)
+        else:
+            sbuf[c] = (
+                pbuf[c, 1 - side, core].astype(F32) + rbuf[c, 1 - side].astype(F32)
+            ).astype(BF16)
+        second_copy(c).start()
+
+    for c in range(CHUNKS):
+        part = jnp.dot(lhs[...], wbuf[:, c * COLS : (c + 1) * COLS], preferred_element_type=F32)
+        pbuf[c] = part.astype(BF16).reshape(2, 2, TOK // 4, COLS)
+        first_copy(c).start()
+        if c > 0:
+            second(c - 1)
+    second(CHUNKS - 1)
 
     def page_wait(k, _):
         source = (me + 64 - k) % 64
@@ -369,75 +486,25 @@
     res_a = jnp.exp2(res_m - both)
     pool_a = jnp.exp2(pool_m - both)
     dec = (res_o * res_a + pool_o * pool_a) / (res_l * res_a + pool_l * pool_a)
-    for h in range(8):
-        lhs[TOK : TOK + 16, h * HD : (h + 1) * HD] = dec[h * 16 : (h + 1) * 16, :].astype(BF16)
-
-    for k in range(1, NR):
-        o_copy(k).wait()
-        st_copy(k).wait()
-    lse = [stbuf[0]] + [strecv[k] for k in range(1, NR)]
-    top = functools.reduce(jnp.maximum, lse)
-    share = [jnp.exp2(a - top) for a in lse]
-    whole = 1.0 / functools.reduce(jnp.add, share)
-    share = [a * whole for a in share]
-    for h in range(8):
-        head, g = h // GROUP, h % GROUP
-        cols = slice(g * TOK, (g + 1) * TOK)
-        merged = obuf[0, head, :, cols].astype(F32) * share[0][h : h + 1]
-        for k in range(1, NR):
-            merged = merged + orecv[k, head, :, cols].astype(F32) * share[k][h : h + 1]
-        lhs[:TOK, h * HD : (h + 1) * HD] = merged.T.astype(BF16)
-
-    core = tp % 2
-    side = tp // 2
-    sibling = side * 2 + (1 - core)
-    across = (1 - side) * 2 + core
-    local[9].wait()
-
-    def first_copy(c):
-        if c == CHUNKS:
-            return remote(pdec.at[:, 1 - core], rdec, t1_s.at[c], t1_r.at[c], tp=sibling)
-        return remote(pbuf.at[c, :, 1 - core], rbuf.at[c], t1_s.at[c], t1_r.at[c], tp=sibling)
-
-    def second_copy(c):
-        if c == CHUNKS:
-            return remote(sdec, tdec, t2_s.at[c], t2_r.at[c], tp=across)
-        return remote(sbuf.at[c], tbuf.at[c], t2_s.at[c], t2_r.at[c], tp=across)
-
-    def second(c):
-        first_copy(c).wait_recv()
-        if c == CHUNKS:
-            sdec[...] = (
-                pdec[1 - side, core].astype(F32) + rdec[1 - side].astype(F32)
-            ).astype(BF16)
-        else:
-            sbuf[c] = (
-                pbuf[c, 1 - side, core].astype(F32) + rbuf[c, 1 - side].astype(F32)
-            ).astype(BF16)
-        second_copy(c).start()
-
-    dec_parts = []
-    for c in range(CHUNKS):
-        part = jnp.dot(lhs[...], wbuf[:, c * COLS : (c + 1) * COLS], preferred_element_type=F32)
-        pbuf[c] = part[:TOK].astype(BF16).reshape(2, 2, TOK // 4, COLS)
-        dec_parts.append(part[TOK:])
-        first_copy(c).start()
-        if c > 0:
-            second(c - 1)
+    dec = jnp.concatenate([dec[h * 16 : (h + 1) * 16] for h in range(8)], axis=1).astype(BF16)
+    dec_parts = [
+        jnp.dot(dec, wbuf[:, c * COLS : (c + 1) * COLS], preferred_element_type=F32)
+        for c in range(CHUNKS)
+    ]
     for t in range(4):
         rows = jnp.concatenate([part[t * 4 : (t + 1) * 4] for part in dec_parts], axis=0)
         pdec[t // 2, t % 2] = rows.astype(BF16)
     first_copy(CHUNKS).start()
-    second(CHUNKS - 1)
-    second(CHUNKS)
     for c in range(CHUNKS):
         second_copy(c).wait_recv()
         out_ref[:, c * COLS : (c + 1) * COLS] = (
             pbuf[c, side, core].astype(F32) + rbuf[c, side].astype(F32) + tbuf[c].astype(F32)
         ).astype(BF16)
+        if c == 1:
+            second(CHUNKS)
     second_copy(CHUNKS).wait_recv()
     rows = pdec[side, core].astype(F32) + rdec[side].astype(F32) + tdec[...].astype(F32)
-    dout_ref[...] = jnp.concatenate(
+    dout_ref[0] = jnp.concatenate(
         [rows[c * 4 : (c + 1) * 4] for c in range(CHUNKS)], axis=1
     ).astype(BF16)
 
@@ -449,9 +516,23 @@
     for k in range(1, NR):
         for head in range(2):
             q_copy(k, head).wait_send()
+    for i in range(MESSAGES):
+        for copy in messages(i):
+            copy.wait_send()
     for c in range(CHUNKS + 1):
         first_copy(c).wait_send()
         second_copy(c).wait_send()
+
+
+def hand_out(out_in, dout_in, out_ref, dout_ref, sem):
+    copies = [
+        pltpu.make_async_copy(out_in, out_ref, sem.at[0]),
+        pltpu.make_async_copy(dout_in, dout_ref, sem.at[1]),
+    ]
+    for copy in copies:
+        copy.start()
+    for copy in copies:
+        copy.wait()
 
 
 def body(
@@ -467,7 +548,7 @@
         name="layer",
         out_shape=[
             jax.ShapeDtypeStruct((TOK // 4, CHUNKS * COLS), BF16),
-            jax.ShapeDtypeStruct((4, CHUNKS * COLS), BF16),
+            jax.ShapeDtypeStruct((1, 4, CHUNKS * COLS), BF16),
         ],
         in_specs=[smem] * 2 + [hbm] * 10,
         out_specs=[vmem, vmem],
@@ -487,15 +568,17 @@
             pltpu.VMEM((NR, 2, HD + 8, QROWS), F32),
             pltpu.VMEM((NR, 2, 8, QROWS), F32),
             pltpu.VMEM((NR, 2, HD, QROWS), BF16),
-            pltpu.VMEM((NR, 2, HD, QROWS), BF16),
-            pltpu.VMEM((NR, 8, TOK), F32),
-            pltpu.VMEM((NR, 8, TOK), F32),
+            pltpu.VMEM((MESSAGES, HD, QROWS), BF16),
+            pltpu.VMEM((NR, 2, 8, TOK), F32),
+            pltpu.VMEM((MESSAGES, 8, TOK), F32),
+            pltpu.VMEM((4, HD, QROWS), BF16),
+            pltpu.VMEM((4, 8, TOK), F32),
             pltpu.VMEM((64, PAGE_ROWS, HD), BF16),
             pltpu.VMEM((64, 2 * PAGE_ROWS, HD), BF16),
             pltpu.VMEM((64, 2 * PAGE_ROWS, HD), BF16),
             pltpu.VMEM((4 * 2048, HD), BF16),
             pltpu.VMEM((8 * HD, CHUNKS * COLS), BF16),
-            pltpu.VMEM((TOK + 16, 8 * HD), BF16),
+            pltpu.VMEM((TOK, 8 * HD), BF16),
             pltpu.VMEM((CHUNKS, 2, 2, TOK // 4, COLS), BF16),
             pltpu.VMEM((CHUNKS, 2, TOK // 4, COLS), BF16),
             pltpu.VMEM((CHUNKS, TOK // 4, COLS), BF16),
@@ -507,8 +590,8 @@
             dma((12,)),
             dma((2, 4, 2)), dma((2, 4, 2)),
             dma((NR, 2)), dma((NR, 2)),
-            dma((NR,)), dma((NR,)),
-            dma((NR,)), dma((NR,)),
+            dma((MESSAGES,)), dma((MESSAGES,)),
+            dma((MESSAGES,)), dma((MESSAGES,)),
             dma((64,)), dma((64,)),
             dma((CHUNKS + 1,)), dma((CHUNKS + 1,)),
             dma((CHUNKS + 1,)), dma((CHUNKS + 1,)),
@@ -523,7 +606,15 @@
         decode_cache.reshape(4 * 2048, HD), decode_q.reshape(128, HD), decode_kv.reshape(64, HD),
         out_weight.reshape(8 * HD, CHUNKS * COLS),
     )
-    return out, dout.reshape(1, 4, CHUNKS * COLS)
+    return pl.pallas_call(
+        hand_out,
+        name="results",
+        out_shape=[jax.ShapeDtypeStruct(a.shape, a.dtype) for a in (out, dout)],
+        in_specs=[hbm, hbm],
+        out_specs=[hbm, hbm],
+        scratch_shapes=[dma((2,))],
+        compiler_params=pltpu.CompilerParams(vmem_limit_bytes=56 << 20),
+    )(out, dout)
 
 
 def solution(mesh):

time: 96.7 us -> 96.4 us (level)
  local copies, waits for them, and re-layouts: 3.05 us -> 0 us
  Pallas kernels: 92.8 us -> 95.7 us
    pallas_call x0 -> x1, Pallas kernels: none -> 10.1 us  [body(): pl.pallas_call(hand_out, name='results', out_shape=[jax.ShapeDtypeStruct(...]
    pallas_call x1, Pallas kernels: 92.8 us -> 85.6 us  [body(): pl.pallas_call(kernel, name='layer', out_shape=[jax.ShapeDtypeStruct((TOK...]
    unnamed x2 -> x0, local copies, waits for them, and re-layouts: 3.05 us -> none
where the time goes in v3:
time: 96.4 us; the launch traced here: 96.3 us
  Pallas kernels  95.7 us (99%)
    pallas_call x1, Pallas kernels, body(): pl.pallas_call(kernel, name='layer', out_shape=[jax.ShapeDtypeStruct((TOK...  85.6 us
    pallas_call x1, Pallas kernels, body(): pl.pallas_call(hand_out, name='results', out_shape=[jax.ShapeDtypeStruct(...  10.1 us

profile of v3, /device:TPU:1, one launch (start us, length us, event | category | flops | bytes accessed | tf_op | source)
XLA Modules:
  0.0 96.3 jit_solution(9213944343962097652)
XLA Ops:
  0.6 85.6 %layer.1 = (bf16[32,4096]{1,0:T(8,128)(2,1)}, bf16[1,4,4096]{2,1,0:T(4,128)(2,1)}) custom-call(s32[64]{0:T(128)} %blocks_ref.1, s32[4]{0:T(128)} %lens_ref.1, bf16[1024,128]{1,0:T(8,128)(2,1)} %bitcast.13, bf16[512,128]{1,0:T(8,128)(2,1)} %bitcast.14, bf16[512,128]{1,0:T(8,128)(2,1)} %bitcast.15, bf16[64,32,128]{2,1,0:T(8,128)(2,1)} %bitcast.12, ...), custom_call_target="tpu_custom_call" | custom-call | tf_op jit(solution)/shard_map/layer/pallas_call | solution.py:546
  86.3 10.1 %results.1 = (bf16[32,4096]{1,0:T(8,128)(2,1)}, bf16[1,4,4096]{2,1,0:T(4,128)(2,1)}) custom-call(bf16[32,4096]{1,0:T(8,128)(2,1)} %get-tuple-element.4.out_in, bf16[1,4,4096]{2,1,0:T(4,128)(2,1)} %get-tuple-element.5.dout_in), custom_call_target="tpu_custom_call" | custom-call | tf_op jit(solution)/shard_map/results/pallas_call | solution.py:609

commit v4 on v3

--- a/solution.py
+++ b/solution.py
@@ -44,7 +44,7 @@
     blocks_ref, lens_ref, q_in, cache_in, span_in, pages_in, dest_in, req_in, dcache_in, dq_in, dkv_in, w_in,
     out_ref, dout_ref,
     q_raw, kv_raw, dest, req, dq_raw, dkv, page_ix, page_at, hide,
-    kvbuf, qbuf, s_ref, acc, peaks, obuf, orecv, stbuf, strecv, mbuf, mst, pages, pg_out, pool, dcache, wbuf,
+    kvbuf, qbuf, s_ref, acc, peaks, obuf, orecv, stbuf, strecv, mbuf, mst, pages, pg_out, pool, pool_bias, dcache, wbuf,
     lhs, pbuf, rbuf, sbuf, tbuf, pdec, rdec, sdec, tdec,
     lsem, kv_s, kv_r, q_s, q_r, o_s, o_r, st_s, st_r, pg_s, pg_r, t1_s, t1_r, t2_s, t2_r,
 ):
@@ -214,6 +214,13 @@
     res_o = jnp.dot(res_p[:, 2048:2112], dkv[...], preferred_element_type=F32)
     for r in range(4):
         res_o = res_o + jnp.where(col_req == r, part[:, r * HD : (r + 1) * HD], 0.0)
+
+    at = lax.broadcasted_iota(jnp.int32, (128, POOL), 1)
+    slot_at = (at // 32) % 2 * 64 + (at // 64) % 2 * 32 + at // 128
+    spread = (lax.broadcasted_iota(jnp.int32, (128, POOL), 0) == slot_at).astype(BF16)
+    mine = lax.dot_general(owned, spread, (((0,), (0,)), ((), ())), preferred_element_type=F32)
+    at = lax.broadcasted_iota(jnp.int32, (1, POOL), 1)
+    pool_bias[...] = jnp.where((mine > 0.5) & (at % 4 == col_head * 2), 0.0, NEG)
 
     q_copy(1, 0).wait_recv()
     for k in (5, 6, 7):
@@ -474,12 +481,7 @@
     own_pages.wait()
     pool_rows = pool[...].reshape(POOL, HD)
     found = lax.dot_general(dq, pool_rows, NT, preferred_element_type=F32)
-    at = lax.broadcasted_iota(jnp.int32, (128, POOL), 1)
-    slot_at = (at // 32) % 2 * 64 + (at // 64) % 2 * 32 + at // 128
-    spread = (lax.broadcasted_iota(jnp.int32, (128, POOL), 0) == slot_at).astype(BF16)
-    mine = lax.dot_general(owned, spread, (((0,), (0,)), ((), ())), preferred_element_type=F32)
-    at = lax.broadcasted_iota(jnp.int32, (1, POOL), 1)
-    found = jnp.where((mine > 0.5) & (at % 4 == col_head * 2), found, NEG)
+    found = found + pool_bias[...]
     pool_m, pool_l, pool_p = weigh(found)
     pool_o = jnp.dot(pool_p, pool_rows, preferred_element_type=F32)
     both = jnp.maximum(res_m, pool_m)
@@ -524,15 +526,9 @@
         second_copy(c).wait_send()
 
 
-def hand_out(out_in, dout_in, out_ref, dout_ref, sem):
-    copies = [
-        pltpu.make_async_copy(out_in, out_ref, sem.at[0]),
-        pltpu.make_async_copy(dout_in, dout_ref, sem.at[1]),
-    ]
-    for copy in copies:
-        copy.start()
-    for copy in copies:
-        copy.wait()
+def hand_out(out_in, dout_in, out_ref, dout_ref):
+    out_ref[...] = out_in[...]
+    dout_ref[...] = dout_in[...]
 
 
 def body(
@@ -576,6 +572,7 @@
             pltpu.VMEM((64, PAGE_ROWS, HD), BF16),
             pltpu.VMEM((64, 2 * PAGE_ROWS, HD), BF16),
             pltpu.VMEM((64, 2 * PAGE_ROWS, HD), BF16),
+            pltpu.VMEM((128, POOL), F32),
             pltpu.VMEM((4 * 2048, HD), BF16),
             pltpu.VMEM((8 * HD, CHUNKS * COLS), BF16),
             pltpu.VMEM((TOK, 8 * HD), BF16),
@@ -610,9 +607,8 @@
         hand_out,
         name="results",
         out_shape=[jax.ShapeDtypeStruct(a.shape, a.dtype) for a in (out, dout)],
-        in_specs=[hbm, hbm],
-        out_specs=[hbm, hbm],
-        scratch_shapes=[dma((2,))],
+        in_specs=[vmem, vmem],
+        out_specs=[vmem, vmem],
         compiler_params=pltpu.CompilerParams(vmem_limit_bytes=56 << 20),
     )(out, dout)
 

time: 96.4 us -> 87.9 us (0.912)
  Pallas kernels: 95.7 us -> 87.2 us
    pallas_call x1, Pallas kernels: 10.1 us -> 1.68 us  [body(): pl.pallas_call(hand_out, name='results', out_shape=[jax.ShapeDtypeStruct(...]
where the time goes in v4:
time: 87.9 us; the launch traced here: 87.8 us
  Pallas kernels  87.2 us (99%)
    pallas_call x1, Pallas kernels, body(): pl.pallas_call(kernel, name='layer', out_shape=[jax.ShapeDtypeStruct((TOK...  85.5 us

profile of v4, /device:TPU:1, one launch (start us, length us, event | category | flops | bytes accessed | tf_op | source)
XLA Modules:
  0.0 87.8 jit_solution(15791375372366922108)
XLA Ops:
  0.6 85.5 %layer.1 = (bf16[32,4096]{1,0:T(8,128)(2,1)}, bf16[1,4,4096]{2,1,0:T(4,128)(2,1)}) custom-call(s32[64]{0:T(128)} %blocks_ref.1, s32[4]{0:T(128)} %lens_ref.1, bf16[1024,128]{1,0:T(8,128)(2,1)} %bitcast.13, bf16[512,128]{1,0:T(8,128)(2,1)} %bitcast.14, bf16[512,128]{1,0:T(8,128)(2,1)} %bitcast.15, bf16[64,32,128]{2,1,0:T(8,128)(2,1)} %bitcast.12, ...), custom_call_target="tpu_custom_call" | custom-call | tf_op jit(solution)/shard_map/layer/pallas_call | solution.py:542
  86.2 1.7 %results.1 = (bf16[32,4096]{1,0:T(8,128)(2,1)}, bf16[1,4,4096]{2,1,0:T(4,128)(2,1)}) custom-call(bf16[32,4096]{1,0:T(8,128)(2,1)} %get-tuple-element.4.out_in, bf16[1,4,4096]{2,1,0:T(4,128)(2,1)} %get-tuple-element.5.dout_in), custom_call_target="tpu_custom_call" | custom-call | tf_op jit(solution)/shard_map/results/pallas_call | solution.py:606

commit v5 on v4

--- a/solution.py
+++ b/solution.py
@@ -19,11 +19,15 @@
 HD = 128
 GROUP = 4
 QROWS = GROUP * TOK
-PHASES = ((0, 1, 7), (2, 6, 3, 5, 4))
+PHASES = ((0, 1, 7), (2, 6), (0, 1, 7, 2, 6), (3, 5, 4))
 MOST_KEYS = 5 * 2 * TOK
 DX = (0, 0, 1, 3, 2, 1, 3, 2)
 DY = (0, 1, 0, 0, 0, 1, 1, 1)
 MESSAGES = 14
+PART = 16
+POOL_EARLY = (0, 3)
+POOL_LATE = (1, 2)
+FIRST_HEAD = 0
 COLS = 1024
 CHUNKS = 4
 PAGE_ROWS = 32
@@ -45,7 +49,7 @@
     out_ref, dout_ref,
     q_raw, kv_raw, dest, req, dq_raw, dkv, page_ix, page_at, hide,
     kvbuf, qbuf, s_ref, acc, peaks, obuf, orecv, stbuf, strecv, mbuf, mst, pages, pg_out, pool, pool_bias, dcache, wbuf,
-    lhs, pbuf, rbuf, sbuf, tbuf, pdec, rdec, sdec, tdec,
+    lhs, pacc, pbuf, rbuf, sbuf, tbuf, pdec, rdec, sdec, tdec,
     lsem, kv_s, kv_r, q_s, q_r, o_s, o_r, st_s, st_r, pg_s, pg_r, t1_s, t1_r, t2_s, t2_r,
 ):
     me = lax.axis_index("ctx")
@@ -175,7 +179,7 @@
         return 0
 
     lax.fori_loop(0, 64, place, 0)
-    own_pages = pltpu.make_async_copy(pg_out.at[me], pool.at[me], lsem.at[11])
+    own_pages = pltpu.make_async_copy(pg_out.at[me], pool.at[0], lsem.at[11])
     own_pages.start()
 
     ring_step(1, 0)
@@ -216,7 +220,8 @@
         res_o = res_o + jnp.where(col_req == r, part[:, r * HD : (r + 1) * HD], 0.0)
 
     at = lax.broadcasted_iota(jnp.int32, (128, POOL), 1)
-    slot_at = (at // 32) % 2 * 64 + (at // 64) % 2 * 32 + at // 128
+    source = (me + 64 - at // 64) % 64
+    slot_at = (at // 32) % 2 * 64 + source % 2 * 32 + source // 2
     spread = (lax.broadcasted_iota(jnp.int32, (128, POOL), 0) == slot_at).astype(BF16)
     mine = lax.dot_general(owned, spread, (((0,), (0,)), ((), ())), preferred_element_type=F32)
     at = lax.broadcasted_iota(jnp.int32, (1, POOL), 1)
@@ -234,7 +239,8 @@
         )
 
     def attend(phase, k, head, slot, own=False):
-        peak = None if phase == 0 else peaks[k, head]
+        start = phase in (0, 2)
+        peak = None if start else peaks[k, head]
         shifts = []
         for i, d in enumerate(PHASES[phase]):
             cached = slice(i * 2 * TOK, (i * 2 + 1) * TOK)
@@ -260,12 +266,13 @@
         values = jnp.concatenate(values, axis=1)
         values = jnp.concatenate([values, jnp.ones((16, values.shape[1]), BF16)], axis=0)
         o = jnp.dot(values, jnp.concatenate(weights, axis=0), preferred_element_type=F32)[: HD + 8]
-        if phase == 0:
+        if not start:
+            before = jnp.max(peaks[k, head], axis=0, keepdims=True) * score_c
+            o = o + acc[k, head] * jnp.exp2(before - m)
+        if phase < 3:
             acc[k, head] = o
             peaks[k, head] = peak
             return
-        before = jnp.max(peaks[k, head], axis=0, keepdims=True) * score_c
-        o = o + acc[k, head] * jnp.exp2(before - m)
         total = o[HD : HD + 1]
         obuf[k, head] = (o[:HD] * (1.0 / total)).astype(BF16)
         lse = m + jnp.log2(total)
@@ -325,15 +332,15 @@
         relay(i - 4, [mine_of(i - 2, 1), came(i - 3)])
         depart(i)
 
-    def step0(k, own=False):
-        scores(0, k, 1, 1)
-        attend(0, k, 0, 0, own)
-        scores(0, (k + 1) % NR, 0, 0)
-        attend(0, k, 1, 1, own)
+    def step(phase, k, later, own=False):
+        scores(phase, k, 1, 1)
+        attend(phase, k, 0, 0, own)
+        scores(phase, later, 0, 0)
+        attend(phase, k, 1, 1, own)
 
     scores(0, 0, 0, 0)
     q_copy(1, 1).wait_recv()
-    step0(0, True)
+    step(0, 0, 1, True)
 
     def first_phase(k, _):
         @pl.when(k == 1)
@@ -358,33 +365,52 @@
         def _():
             ring_step(2, 1)
 
-        for i in (4, 5, 6):
+        step(0, k, (k + 1) % 5)
+        return 0
+
+    lax.fori_loop(1, 5, first_phase, 0)
+    scores(1, 0, 0, 0)
+
+    def middle_phase(k, _):
+        @pl.when(k == 2)
+        def _():
+            ring_step(3, 0)
+
+        step(1, k, (k + 1) % 5)
+        return 0
+
+    lax.fori_loop(0, 5, middle_phase, 0)
+    ring_step(3, 1)
+    q_copy(5, 0).wait_recv()
+    q_copy(5, 1).wait_recv()
+
+    def page_copy(k):
+        to = (me + k) % 64
+        return remote(pg_out.at[to], pool.at[k], pg_s.at[k], pg_r.at[k], ctx=to)
+
+    def page_start(k, _):
+        page_copy(k).start()
+        return 0
+
+    lax.fori_loop(1, 64, page_start, 0)
+
+    scores(2, 5, 0, 0)
+
+    def late_phase(k, _):
+        for i in (5, 6):
             @pl.when(k == i)
             def _():
                 q_copy(i + 1, 0).wait_recv()
                 q_copy(i + 1, 1).wait_recv()
 
-        step0(k)
-        return 0
-
-    lax.fori_loop(1, NR, first_phase, 0)
-    ring_step(3, 0)
-    ring_step(3, 1)
-
-    def page_copy(k):
-        to = (me + k) % 64
-        return remote(pg_out.at[to], pool.at[me], pg_s.at[k], pg_r.at[k], ctx=to)
-
-    def page_start(k, _):
-        page_copy(k).start()
-        return 0
-
-    lax.fori_loop(1, 64, page_start, 0)
-
+        step(2, k, 5 + (k - 4) % 3)
+        return 0
+
+    lax.fori_loop(5, NR, late_phase, 0)
     for t, half, way in ((2, 1, 0), (2, 0, 1), (3, 0, 0), (3, 1, 1)):
         ring(t, half, way).wait_recv()
 
-    scores(1, 1, 0, 0)
+    scores(3, 1, 0, 0)
 
     def second_at(j):
         t = (j + 1) // 3
@@ -392,10 +418,7 @@
 
     def second_phase(j, _):
         k = second_at(j)
-        scores(1, k, 1, 1)
-        attend(1, k, 0, 0)
-        scores(1, second_at(j + 1), 0, 0)
-        attend(1, k, 1, 1)
+        step(3, k, second_at(j + 1))
 
         @pl.when(j == 1)
         def _():
@@ -426,20 +449,42 @@
     depart(13)
     relay_head1(6)
 
-    for head in range(2):
+    def page_wait(k, _):
+        page_copy(k).wait()
+        return 0
+
+    def pool_part(p, state):
+        lax.fori_loop(max(1, p * PART), (p + 1) * PART, page_wait, 0)
+        if p == 0:
+            own_pages.wait()
+        rows = pool[p * PART : (p + 1) * PART].reshape(PART * 64, HD)
+        found = lax.dot_general(dq, rows, NT, preferred_element_type=F32)
+        found = found + pool_bias[:, p * PART * 64 : (p + 1) * PART * 64]
+        m, total, weights = weigh(found)
+        o = jnp.dot(weights, rows, preferred_element_type=F32)
+        both = jnp.maximum(state[0], m)
+        old = jnp.exp2(state[0] - both)
+        new = jnp.exp2(m - both)
+        return both, state[1] * old + total * new, state[2] * old + o * new
+
+    pool_state = (res_m, res_l, res_o)
+    for p in POOL_EARLY:
+        pool_state = pool_part(p, pool_state)
+
+    def collect(head):
         others = (13, 7, 8, 9) if head == 0 else (0, 4, 5, 6)
         for i in others:
             arrive(i)
         merged, _ = merge([mine_of(0, head)] + [came(i) for i in others])
         for g in range(GROUP):
-            h = head * GROUP + g
-            lhs[:, h * HD : (h + 1) * HD] = merged[:, g * TOK : (g + 1) * TOK].T.astype(BF16)
+            lhs[head, :, g * HD : (g + 1) * HD] = merged[:, g * TOK : (g + 1) * TOK].T.astype(BF16)
 
     core = tp % 2
     side = tp // 2
     sibling = side * 2 + (1 - core)
     across = (1 - side) * 2 + core
     local[9].wait()
+    half_width = GROUP * HD
 
     def first_copy(c):
         if c == CHUNKS:
@@ -463,31 +508,25 @@
             ).astype(BF16)
         second_copy(c).start()
 
+    collect(FIRST_HEAD)
     for c in range(CHUNKS):
-        part = jnp.dot(lhs[...], wbuf[:, c * COLS : (c + 1) * COLS], preferred_element_type=F32)
+        weight = wbuf[FIRST_HEAD * half_width : (FIRST_HEAD + 1) * half_width, c * COLS : (c + 1) * COLS]
+        pacc[c] = jnp.dot(lhs[FIRST_HEAD], weight, preferred_element_type=F32)
+    last = 1 - FIRST_HEAD
+    collect(last)
+    for c in range(CHUNKS):
+        weight = wbuf[last * half_width : (last + 1) * half_width, c * COLS : (c + 1) * COLS]
+        part = pacc[c] + jnp.dot(lhs[last], weight, preferred_element_type=F32)
         pbuf[c] = part.astype(BF16).reshape(2, 2, TOK // 4, COLS)
         first_copy(c).start()
         if c > 0:
             second(c - 1)
     second(CHUNKS - 1)
 
-    def page_wait(k, _):
-        source = (me + 64 - k) % 64
-        to = (me + k) % 64
-        remote(pg_out.at[to], pool.at[source], pg_s.at[k], pg_r.at[k], ctx=to).wait()
-        return 0
-
-    lax.fori_loop(1, 64, page_wait, 0)
-    own_pages.wait()
-    pool_rows = pool[...].reshape(POOL, HD)
-    found = lax.dot_general(dq, pool_rows, NT, preferred_element_type=F32)
-    found = found + pool_bias[...]
-    pool_m, pool_l, pool_p = weigh(found)
-    pool_o = jnp.dot(pool_p, pool_rows, preferred_element_type=F32)
-    both = jnp.maximum(res_m, pool_m)
-    res_a = jnp.exp2(res_m - both)
-    pool_a = jnp.exp2(pool_m - both)
-    dec = (res_o * res_a + pool_o * pool_a) / (res_l * res_a + pool_l * pool_a)
+    for p in POOL_LATE:
+        pool_state = pool_part(p, pool_state)
+    own_m, own_l, own_o = pool_state
+    dec = own_o / own_l
     dec = jnp.concatenate([dec[h * 16 : (h + 1) * 16] for h in range(8)], axis=1).astype(BF16)
     dec_parts = [
         jnp.dot(dec, wbuf[:, c * COLS : (c + 1) * COLS], preferred_element_type=F32)
@@ -575,7 +614,8 @@
             pltpu.VMEM((128, POOL), F32),
             pltpu.VMEM((4 * 2048, HD), BF16),
             pltpu.VMEM((8 * HD, CHUNKS * COLS), BF16),
-            pltpu.VMEM((TOK, 8 * HD), BF16),
+            pltpu.VMEM((2, TOK, GROUP * HD), BF16),
+            pltpu.VMEM((CHUNKS, TOK, COLS), F32),
             pltpu.VMEM((CHUNKS, 2, 2, TOK // 4, COLS), BF16),
             pltpu.VMEM((CHUNKS, 2, TOK // 4, COLS), BF16),
             pltpu.VMEM((CHUNKS, TOK // 4, COLS), BF16),

time: 87.9 us -> 85 us (0.967)
  Pallas kernels: 87.2 us -> 84.3 us
    pallas_call x1, Pallas kernels: 85.5 us -> 82.6 us  [body(): pl.pallas_call(kernel, name='layer', out_shape=[jax.ShapeDtypeStruct((TOK...]
where the time goes in v5:
time: 85 us; the launch traced here: 84.9 us
  Pallas kernels  84.3 us (99%)
    pallas_call x1, Pallas kernels, body(): pl.pallas_call(kernel, name='layer', out_shape=[jax.ShapeDtypeStruct((TOK...  82.6 us

profile of v5, /device:TPU:1, one launch (start us, length us, event | category | flops | bytes accessed | tf_op | source)
XLA Modules:
  0.0 84.9 jit_solution(8335887026892836748)
XLA Ops:
  0.6 82.6 %layer.1 = (bf16[32,4096]{1,0:T(8,128)(2,1)}, bf16[1,4,4096]{2,1,0:T(4,128)(2,1)}) custom-call(s32[64]{0:T(128)} %blocks_ref.1, s32[4]{0:T(128)} %lens_ref.1, bf16[1024,128]{1,0:T(8,128)(2,1)} %bitcast.13, bf16[512,128]{1,0:T(8,128)(2,1)} %bitcast.14, bf16[512,128]{1,0:T(8,128)(2,1)} %bitcast.15, bf16[64,32,128]{2,1,0:T(8,128)(2,1)} %bitcast.12, ...), custom_call_target="tpu_custom_call" | custom-call | tf_op jit(solution)/shard_map/layer/pallas_call | solution.py:581
  83.2 1.7 %results.1 = (bf16[32,4096]{1,0:T(8,128)(2,1)}, bf16[1,4,4096]{2,1,0:T(4,128)(2,1)}) custom-call(bf16[32,4096]{1,0:T(8,128)(2,1)} %get-tuple-element.4.out_in, bf16[1,4,4096]{2,1,0:T(4,128)(2,1)} %get-tuple-element.5.dout_in), custom_call_target="tpu_custom_call" | custom-call | tf_op jit(solution)/shard_map/results/pallas_call | solution.py:646

commit v6 on v5

--- a/solution.py
+++ b/solution.py
@@ -435,14 +435,11 @@
             def _():
                 depart(i + 2)
 
-        for i in (6, 7):
-            @pl.when(j == i)
-            def _():
-                relay_head1(i - 2)
-
         return 0
 
     lax.fori_loop(1, NR + 1, second_phase, 0)
+    relay_head1(4)
+    relay_head1(5)
     for i in (10, 11, 12):
         arrive(i)
     relay(3, [mine_of(1, 0), came(10), came(11), came(12)])

time: 85 us -> 85.1 us (level)
  no operation moved by 1% of the time
where the time goes in v6:
time: 85.1 us; the launch traced here: 84.9 us
  Pallas kernels  84.3 us (99%)
    pallas_call x1, Pallas kernels, body(): pl.pallas_call(kernel, name='layer', out_shape=[jax.ShapeDtypeStruct((TOK...  82.6 us

profile of v6, /device:TPU:1, one launch (start us, length us, event | category | flops | bytes accessed | tf_op | source)
XLA Modules:
  0.0 84.9 jit_solution(3444454012962028061)
XLA Ops:
  0.6 82.6 %layer.1 = (bf16[32,4096]{1,0:T(8,128)(2,1)}, bf16[1,4,4096]{2,1,0:T(4,128)(2,1)}) custom-call(s32[64]{0:T(128)} %blocks_ref.1, s32[4]{0:T(128)} %lens_ref.1, bf16[1024,128]{1,0:T(8,128)(2,1)} %bitcast.13, bf16[512,128]{1,0:T(8,128)(2,1)} %bitcast.14, bf16[512,128]{1,0:T(8,128)(2,1)} %bitcast.15, bf16[64,32,128]{2,1,0:T(8,128)(2,1)} %bitcast.12, ...), custom_call_target="tpu_custom_call" | custom-call | tf_op jit(solution)/shard_map/layer/pallas_call | solution.py:578
  83.3 1.7 %results.1 = (bf16[32,4096]{1,0:T(8,128)(2,1)}, bf16[1,4,4096]{2,1,0:T(4,128)(2,1)}) custom-call(bf16[32,4096]{1,0:T(8,128)(2,1)} %get-tuple-element.4.out_in, bf16[1,4,4096]{2,1,0:T(4,128)(2,1)} %get-tuple-element.5.dout_in), custom_call_target="tpu_custom_call" | custom-call | tf_op jit(solution)/shard_map/results/pallas_call | solution.py:643
